TPU v7x, 32 devices: a whole 2x2x4 slice. The times are simulated.
32 devices in a mesh: freq: 8 (over y, x, core), stn: 4 (over z).
Axes of the slice: x: 2, y: 2, z: 4, core: 2. Of those that a mesh axis runs over, the one named last changes fastest.
Arguments:
- visibilities: float32 [8, 8, 256, 256], P('freq', None, 'stn'), may hold values from -6 to 6
- flag_mask: int32 [256, 256], P('stn'), may hold values 0 or 1
- stations: float32 [3, 256], P(None, 'stn'), may hold values from -32 to 32
- directions: float32 [2, 1536], replicated, may hold values from -0.5 to 0.5
- intensity: float32 [1536], replicated, may hold values from 0.02 to 0.2
- polarized: float32 [2, 1536], replicated, may hold values from -0.4375 to 0.4375
- spectral: float32 [1536], replicated, may hold values from -1.5 to 0.5
- clusters: int32 [1536], replicated, may hold values from 0 to 15, as said below
- jones_gains: float32 [8, 8, 16, 256], P('freq', None, None, 'stn'), may hold values from -6 to 6
- scaled_duals: float32 [8, 8, 16, 256], P('freq', None, None, 'stn'), may hold values from -4 to 4
- consensus: float32 [4, 8, 16, 256], P(None, None, None, 'stn'), may hold values from -6 to 6
Outputs:
- jones_next: float32 [8, 8, 16, 256], P('freq', None, None, 'stn')
- duals_next: float32 [8, 8, 16, 256], P('freq', None, None, 'stn')
- consensus_next: float32 [4, 8, 16, 256], P(None, None, None, 'stn')
Inputs may be any that keep to these rules, and one draw needn't show every extreme that they name: `clusters`: every direction holds exactly 96 components.
All inputs are finite; a program needn't handle non-finite values. No bound on the sum of `flag_mask` on one device may be relied on, other than what follows from the above.
Results may differ from a plain program's by a relative error of at most 0.0019.
Values may be sent and summed in bfloat16 or wider, within the bound.
A program may use at most 64 MiB of HBM per device.

v0:
```python
import jax
import jax.numpy as jnp
from jax import lax
from jax.sharding import PartitionSpec as P

DIRS = 16


TWO_PI = 6.283185307179586
PENALTY = 40.0
STEP_SIZE = 0.5


def complex_mul(lhs_value, rhs_value):
    return (
        lhs_value[0] * rhs_value[0] - lhs_value[1] * rhs_value[1],
        lhs_value[0] * rhs_value[1] + lhs_value[1] * rhs_value[0],
    )


def complex_add(lhs_value, rhs_value):
    return (lhs_value[0] + rhs_value[0], lhs_value[1] + rhs_value[1])


def complex_conj(number):
    return (number[0], -number[1])


def matrix_mul(lhs_matrix, rhs_matrix):
    return [
        complex_add(
            complex_mul(lhs_matrix[0], rhs_matrix[0]), complex_mul(lhs_matrix[1], rhs_matrix[2])
        ),
        complex_add(
            complex_mul(lhs_matrix[0], rhs_matrix[1]), complex_mul(lhs_matrix[1], rhs_matrix[3])
        ),
        complex_add(
            complex_mul(lhs_matrix[2], rhs_matrix[0]), complex_mul(lhs_matrix[3], rhs_matrix[2])
        ),
        complex_add(
            complex_mul(lhs_matrix[2], rhs_matrix[1]), complex_mul(lhs_matrix[3], rhs_matrix[3])
        ),
    ]


def matrix_herm(matrix):
    return [
        complex_conj(matrix[0]),
        complex_conj(matrix[2]),
        complex_conj(matrix[1]),
        complex_conj(matrix[3]),
    ]


def unpack_matrix(stacked):
    return [
        (stacked[0], stacked[1]),
        (stacked[2], stacked[3]),
        (stacked[4], stacked[5]),
        (stacked[6], stacked[7]),
    ]


def pack_matrix(matrix):
    return jnp.stack([member for element in matrix for member in element])


def summed_pack(matrix, reduce_dim):
    return -jnp.stack([jnp.sum(member, reduce_dim) for element in matrix for member in element])


def band_ratio(index_value, band_count):
    return 0.5 + 3.0 * (index_value.astype(jnp.float32) + 0.5) / band_count


def station_table(positions, sky_dirs, freq_ratio):
    dir_l = sky_dirs[0][None, :]
    dir_m = sky_dirs[1][None, :]
    dir_n = jnp.sqrt(1.0 - dir_l * dir_l - dir_m * dir_m)
    geometry = (
        dir_l * positions[0][:, None]
        + dir_m * positions[1][:, None]
        + (dir_n - 1.0) * positions[2][:, None]
    )
    phase_angle = TWO_PI * freq_ratio * geometry
    return jnp.stack([jnp.cos(phase_angle), -jnp.sin(phase_angle)]).astype(jnp.bfloat16)


def flux_weights(intensity, polarized, spectral, freq_ratio):
    factor = jnp.power(freq_ratio, spectral)
    return jnp.stack(
        [
            (intensity + polarized[0]) * factor,
            polarized[1] * factor,
            (intensity - polarized[0]) * factor,
        ]
    )


def legendre_table(band_count):
    centre = (2.0 * jnp.arange(band_count, dtype=jnp.float32) + 1.0) / band_count - 1.0
    return jnp.stack(
        [
            jnp.ones_like(centre),
            centre,
            0.5 * (3.0 * centre * centre - 1.0),
            0.5 * (5.0 * centre * centre * centre - 3.0 * centre),
        ],
        axis=1,
    )


def gram_solve(gram_matrix, rhs_rows):
    chol_lower = jnp.linalg.cholesky(gram_matrix)
    forward = []
    for row_at in range(4):
        current = rhs_rows[row_at]
        for col_at in range(row_at):
            current = current - chol_lower[row_at, col_at] * forward[col_at]
        forward.append(current / chol_lower[row_at, row_at])
    backward = [forward[0]] * 4
    for row_at in (3, 2, 1, 0):
        current = forward[row_at]
        for col_at in range(row_at + 1, 4):
            current = current - chol_lower[col_at, row_at] * backward[col_at]
        backward[row_at] = current / chol_lower[row_at, row_at]
    return jnp.stack(backward)


def coherence(direction, own_table, all_table, weights, block_span):
    offset = direction * block_span
    own_real = lax.dynamic_slice_in_dim(own_table[0], offset, block_span, 1)
    own_imag = lax.dynamic_slice_in_dim(own_table[1], offset, block_span, 1)
    weight_block = lax.dynamic_slice_in_dim(weights, offset, block_span, 1)
    blocks = []
    for flux_at in range(3):
        factor_row = weight_block[flux_at][None, :]
        blocks.append(
            jnp.concatenate([own_real * factor_row, own_imag * factor_row], 1).astype(jnp.bfloat16)
        )
    operand_left = jnp.concatenate(blocks, 0)
    far_real = lax.dynamic_slice_in_dim(all_table[0], offset, block_span, 1)
    far_imag = lax.dynamic_slice_in_dim(all_table[1], offset, block_span, 1)
    operand_right = jnp.concatenate(
        [jnp.concatenate([far_real, far_imag], 1), jnp.concatenate([-far_imag, far_real], 1)], 0
    )
    product = lax.dot_general(
        operand_left, operand_right, (((1,), (1,)), ((), ())), preferred_element_type=jnp.float32
    )
    row_count = own_real.shape[0]
    col_count = far_real.shape[0]
    entries = [
        (
            product[flux_at * row_count : (flux_at + 1) * row_count, :col_count],
            product[flux_at * row_count : (flux_at + 1) * row_count, col_count:],
        )
        for flux_at in range(3)
    ]
    return [entries[0], entries[1], entries[1], entries[2]]


def residual_of(
    band_vis, mask_float, near_gains, far_gains, own_table, all_table, weights, block_span
):

    def residual_direction_step(model_sum, direction):
        coh_matrix = coherence(direction, own_table, all_table, weights, block_span)
        near_jones = unpack_matrix(
            lax.dynamic_index_in_dim(near_gains, direction, 1, keepdims=False)[:, :, None]
        )
        far_jones = unpack_matrix(
            lax.dynamic_index_in_dim(far_gains, direction, 1, keepdims=False)[:, None, :]
        )
        model_term = matrix_mul(matrix_mul(near_jones, coh_matrix), matrix_herm(far_jones))
        return (model_sum + pack_matrix(model_term), None)

    model_sum, _ = lax.scan(
        residual_direction_step,
        jnp.zeros(band_vis.shape, jnp.float32),
        jnp.arange(near_gains.shape[1], dtype=jnp.int32),
    )
    return (band_vis - model_sum) * mask_float[None]


def gradient_of(residual, near_gains, far_gains, own_table, all_table, weights, block_span):
    res_matrix = unpack_matrix(residual)

    def gradient_direction_step(state_value, direction):
        coh_matrix = coherence(direction, own_table, all_table, weights, block_span)
        near_jones = unpack_matrix(
            lax.dynamic_index_in_dim(near_gains, direction, 1, keepdims=False)[:, :, None]
        )
        far_jones = unpack_matrix(
            lax.dynamic_index_in_dim(far_gains, direction, 1, keepdims=False)[:, None, :]
        )
        col_part = matrix_mul(matrix_herm(res_matrix), matrix_mul(near_jones, coh_matrix))
        row_part = matrix_mul(res_matrix, matrix_mul(far_jones, matrix_herm(coh_matrix)))
        return (state_value, (summed_pack(row_part, 1), summed_pack(col_part, 0)))

    _, (row_terms, col_terms) = lax.scan(
        gradient_direction_step,
        jnp.zeros((), jnp.float32),
        jnp.arange(near_gains.shape[1], dtype=jnp.int32),
    )
    return (row_terms, col_terms)


def local(
    visibilities,
    flag_mask,
    stations,
    directions,
    intensity,
    polarized,
    spectral,
    clusters,
    jones_gains,
    scaled_duals,
    consensus,
):
    band_count = lax.axis_size("freq")
    band_index = lax.axis_index("freq")
    block_count = lax.axis_size("stn")
    sort_order = jnp.argsort(clusters, stable=True)
    sky_dirs = directions[:, sort_order]
    sky_flux = intensity[sort_order]
    sky_pol = polarized[:, sort_order]
    sky_index = spectral[sort_order]
    block_span = clusters.shape[0] // DIRS
    freq_ratio = band_ratio(band_index, band_count)
    weights = flux_weights(sky_flux, sky_pol, sky_index, freq_ratio)
    own_gains = jones_gains[0]
    own_duals = scaled_duals[0]
    station_rows = own_gains.shape[2]
    own_table = station_table(stations, sky_dirs, freq_ratio)
    all_table = lax.all_gather(own_table, "stn", axis=1, tiled=True)
    all_gains = lax.all_gather(own_gains, "stn", axis=2, tiled=True)
    residual = residual_of(
        visibilities[0],
        flag_mask.astype(jnp.float32),
        own_gains,
        all_gains,
        own_table,
        all_table,
        weights,
        block_span,
    )
    row_terms, col_terms = gradient_of(
        residual, own_gains, all_gains, own_table, all_table, weights, block_span
    )
    basis_table = legendre_table(band_count)
    basis_row = lax.dynamic_index_in_dim(basis_table, band_index, 0, keepdims=False)
    poly_value = jnp.sum(basis_row[:, None, None, None] * consensus, 0)
    penalty_term = PENALTY / 2.0 * (own_gains - poly_value + own_duals)
    own_columns = lax.psum_scatter(col_terms, "stn", scatter_dimension=2, tiled=True)
    drive = jnp.transpose(row_terms + own_columns, (1, 0, 2)) + penalty_term
    total_sq = lax.psum(jnp.sum(drive * drive), "stn")
    entry_count = drive.shape[0] * drive.shape[1] * station_rows * block_count
    step_length = STEP_SIZE / jnp.sqrt(total_sq / entry_count + 1e-06)
    jones_next = own_gains - step_length * drive
    weighted_sum = basis_row[:, None, None, None] * (jones_next + own_duals)[None]
    summed = lax.psum(weighted_sum, "freq")
    gram_matrix = jnp.dot(basis_table.T, basis_table, precision=lax.Precision.HIGHEST)
    consensus_next = gram_solve(gram_matrix, summed.reshape(4, -1)).reshape(summed.shape)
    poly_next = jnp.sum(basis_row[:, None, None, None] * consensus_next, 0)
    duals_next = own_duals + jones_next - poly_next
    return (jones_next[None], duals_next[None], consensus_next)


def solution(mesh):
    placed = (
        P("freq", None, "stn", None),
        P("stn", None),
        P(None, "stn"),
        P(),
        P(),
        P(),
        P(),
        P(),
        P("freq", None, None, "stn"),
        P("freq", None, None, "stn"),
        P(None, None, None, "stn"),
    )
    return jax.shard_map(
        local,
        mesh=mesh,
        in_specs=placed,
        out_specs=(
            P("freq", None, None, "stn"),
            P("freq", None, None, "stn"),
            P(None, None, None, "stn"),
        ),
        check_vma=False,
    )
```

profile of v0, /device:TPU:0, one launch (start us, length us, event | category | flops | bytes accessed | tf_op | source)
XLA Modules:
  0.0 491.2 jit_solution(10701476802847450852)
XLA Ops:
  9.0 5.7 %sort.17 = (s32[1536]{0:T(1024)}, s32[1536]{0:T(1024)S(1)}) sort(s32[1536]{0:T(1024)} %param.22, s32[1536]{0:T(1024)S(1)} %iota.46), dimensions={0}, to_apply=%region_0.0 | sort | flops 16896 | bytes 24576 | tf_op jit(solution)/shard_map/jit(argsort)/sort | solution.py:224
  14.8 2.6 gather_fusion
  17.7 1.7 cosine_convert_fusion
  21.3 36.1 %all-gather = f32[1,8,16,256]{2,1,0,3:T(8,128)S(1)} all-gather(f32[1,8,16,64]{2,1,0,3:T(8,128)S(1)} %copy.49), channel_id=2, replica_groups=mesh['freq'=8,'stn'=4] {'stn'}, dimensions={3}, use_global_device_ids=true | all-gather | bytes 163840 | tf_op jit(solution)/shard_map/all_gather | solution.py:237
  58.4 8.4 %gather_fusion.1 = f32[1536]{0:T(1024)S(1)} fusion(f32[1536]{0:T(1024)S(1)} %copy-done, s32[2048]{0:T(1024)S(1)} %pad_clamp_fusion), kind=kCustom, calls=%fused_computation.1 | custom fusion | bytes 18432 | tf_op jit(solution)/shard_map/gather | solution.py:226
  66.8 8.4 %gather_fusion.3 = f32[1536]{0:T(1024)S(1)} fusion(f32[1536]{0:T(1024)S(1)} %copy-done.1, s32[2048]{0:T(1024)S(1)} %pad_clamp_fusion), kind=kCustom, calls=%fused_computation.3 | custom fusion | bytes 18432 | tf_op jit(solution)/shard_map/gather | solution.py:228
  75.5 2.6 gather_fusion.2
  81.2 134.0 %while.25 = (s32[]{:T(128)}, f32[8,64,256]{2,1,0:T(8,128)S(1)}, s32[16]{0:T(128)S(1)}, f32[8,16,64]{2,1,0:T(8,128)}, bf16[2,64,1536]{2,1,0:T(8,128)(2,1)S(1)}, /...) while((s32[]{:T(128)}, f32[8,64,256]{2,1,0:T(8,128)S(1)}, ...), condition=%wide.region_2.3_spmd.clone, body=%wide.region_1.2_spmd.clone.sunk | while | flops 41235472 | bytes 9933895 | solution.py:177
  84.5 1.5 fusion.128
  92.9 1.5 fusion.128
  101.3 1.5 fusion.128
  109.6 1.5 fusion.128
  118.0 1.5 fusion.128
  126.4 1.5 fusion.128
  134.8 1.5 fusion.128
  143.1 1.5 fusion.128
  151.5 1.5 fusion.128
  159.9 1.5 fusion.128
  168.2 1.5 fusion.128
  176.6 1.5 fusion.128
  185.0 1.5 fusion.128
  193.4 1.5 fusion.128
  201.7 1.5 fusion.128
  210.1 1.5 fusion.128
  217.3 168.0 %while.24 = (s32[]{:T(128)}, f32[16,8,64]{2,0,1:T(8,128)}, f32[16,8,256]{2,1,0:T(8,128)}, s32[16]{0:T(128)}, f32[8,16,256]{2,1,0:T(8,128)}, /*index=5*/bf16[2,64...) while((s32[]{:T(128)}, f32[16,8,64]{2,0,1:T(8,128)}, ...), condition=%wide.region_20.21_spmd, body=%wide.region_3.20_spmd.sunk | while | flops 43200516 | bytes 13513497 | solution.py:200
  224.4 1.4 dynamic_update_slice.14
  234.9 1.4 dynamic_update_slice.14
  245.4 1.4 dynamic_update_slice.14
  255.9 1.4 dynamic_update_slice.14
  266.4 1.4 dynamic_update_slice.14
  276.9 1.4 dynamic_update_slice.14
  287.4 1.4 dynamic_update_slice.14
  297.9 1.4 dynamic_update_slice.14
  308.4 1.4 dynamic_update_slice.14
  318.9 1.4 dynamic_update_slice.14
  329.4 1.4 dynamic_update_slice.14
  339.9 1.4 dynamic_update_slice.14
  350.4 1.4 dynamic_update_slice.14
  361.0 1.4 dynamic_update_slice.14
  371.4 1.4 dynamic_update_slice.14
  381.9 1.4 dynamic_update_slice.14
  385.4 1.4 copy.59
  389.1 19.8 %reduce-scatter.4.cloned.1.call-done = f32[64,128]{1,0:T(8,128)} async-done(((f32[256,128]{1,0:T(8,128)}), f32[64,128]{1,0:T(8,128)}) %reduce-scatter.4.cloned.1.call-update) | async-done | bytes 32784
  409.9 1.5 multiply_reduce_fusion.2
  411.4 9.4 %psum.14 = f32[]{:T(128)} all-reduce(f32[]{:T(128)} %get-tuple-element.475), channel_id=1, replica_groups=mesh['freq'=8,'stn'=4] {'stn'}, use_global_device_ids=true, to_apply=%region_24.25 | all-reduce | flops 1 | bytes 8 | tf_op jit(solution)/shard_map/psum | solution.py:257
  421.5 1.5 bitcast_add_fusion
  425.8 50.8 %all-reduce.2.cloned.1.call-done = f32[4,8,16,64]{3,2,1,0:T(8,128)} async-done(((f32[4,8,16,64]{3,2,1,0:T(8,128)}), f32[4,8,16,64]{3,2,1,0:T(8,128)}) %all-reduce.2.cloned.1.call-update) | async-done | bytes 131088 | tf_op jit(solution)/shard_map/psum | solution.py:262
  476.7 6.6 %subtract_divide_fusion = (f32[1,8,16,64]{3,2,1,0:T(8,128)S(1)}, f32[1,8,16,64]{3,2,1,0:T(8,128)S(1)}, f32[1,8,16,64]{3,2,1,0:T(8,128)S(1)}, f32[1,8,16,64]{3,2,1,0:T(8,128)S(1)}) fusion(f32[]{:T(128)} %bitcast.70, f32[]{:T(128)} %bitcast.67, f32[]{:T(128)} %bitcast.64, f32[]{:T(128)} %bitcast.63, f32[4,8,16,64]{3,2,1,0:T(8,128)} %all-reduce.2.cloned.1.call-done, ...), kind=kLoop, calls=%fused_computation.215 | loop fusion | flops 253952 | bytes 262184 | tf_op jit(solution)/shard_map/div | solution.py:126
  (1163 shorter events, 182.9 us)
Async XLA Ops:
  7.2 51.2 %copy-start = (f32[1536]{0:T(1024)S(1)}, f32[1536]{0:T(1024)}, u32[]{:S(2)}) copy-start(f32[1536]{0:T(1024)} %param.19) | copy-start | bytes 18436
  7.2 74.0 %all-gather.3.cloned.1.call-start = ((), (), s32[]{:S(2)}) async-start(), calls=%async_computation.1 | async-start | bytes 1966080 | tf_op jit(solution)/shard_map/all_gather | solution.py:236
  20.2 388.7 %reduce-scatter.4.cloned.1.call-start = ((), (), s32[]{:S(2)}) async-start(), calls=%async_computation.3 | async-start | bytes 163840
  58.4 8.4 %copy-start.1 = (f32[1536]{0:T(1024)S(1)}, f32[1536]{0:T(1024)}, u32[]{:S(2)}) copy-start(f32[1536]{0:T(1024)} %param.21) | copy-start | bytes 18436
  66.8 8.4 %copy-start.22 = (f32[2,1536]{1,0:T(2,128)S(1)}, f32[2,1536]{1,0:T(2,128)}, u32[]{:S(2)}) copy-start(f32[2,1536]{1,0:T(2,128)} %param.20) | copy-start | bytes 36868
  75.2 4.6 copy-start.17
  75.2 6.0 %copy-start.3 = (bf16[2,64,1536]{2,1,0:T(8,128)(2,1)S(1)}, bf16[2,64,1536]{2,1,0:T(8,128)(2,1)}, u32[]{:S(2)}) copy-start(bf16[2,64,1536]{2,1,0:T(8,128)(2,1)} %pad_maximum_fusion) | copy-start | bytes 1179652
  81.2 134.0 %copy-start.16 = (f32[1,8,64,256]{3,2,1,0:T(8,128)S(1)}, f32[1,8,64,256]{3,2,1,0:T(8,128)}, u32[]{:S(2)}) copy-start(f32[1,8,64,256]{3,2,1,0:T(8,128)} %param.15) | copy-start | bytes 1572868
  241.5 3.6 copy-start.4
  241.5 3.6 copy-start.5
  241.5 3.6 copy-start.6
  241.5 3.6 copy-start.7
  241.5 3.6 copy-start.8
  241.5 3.6 copy-start.9
  241.5 3.6 copy-start.10
  241.6 3.6 copy-start.11
  252.0 3.6 copy-start.4
  252.0 3.6 copy-start.5
  252.0 3.6 copy-start.6
  252.0 3.6 copy-start.7
  252.0 3.6 copy-start.8
  252.0 3.6 copy-start.9
  252.0 3.6 copy-start.10
  252.1 3.6 copy-start.11
  262.5 3.6 copy-start.4
  262.5 3.6 copy-start.5
  262.5 3.6 copy-start.6
  262.5 3.6 copy-start.7
  262.5 3.6 copy-start.8
  262.5 3.6 copy-start.9
  262.6 3.6 copy-start.10
  262.6 3.6 copy-start.11
  273.0 3.6 copy-start.4
  273.0 3.6 copy-start.5
  273.0 3.6 copy-start.6
  273.0 3.6 copy-start.7
  273.0 3.6 copy-start.8
  273.1 3.6 copy-start.9
  273.1 3.6 copy-start.10
  273.1 3.6 copy-start.11
  304.5 3.6 copy-start.4
  304.5 3.6 copy-start.5
  304.5 3.6 copy-start.6
  304.5 3.6 copy-start.7
  385.4 24.5 %copy-start.18 = (f32[1,8,16,64]{3,2,1,0:T(8,128)S(1)}, f32[1,8,16,64]{3,2,1,0:T(8,128)}, u32[]{:S(2)}) copy-start(f32[1,8,16,64]{3,2,1,0:T(8,128)} %param.24) | copy-start | bytes 98308
  385.4 24.5 %copy-start.19 = (f32[8,16,64]{2,1,0:T(8,128)S(1)}, f32[8,16,64]{2,1,0:T(8,128)}, u32[]{:S(2)}) copy-start(f32[8,16,64]{2,1,0:T(8,128)} %multiply_reduce_fusion.1) | copy-start | bytes 98308
  385.4 24.5 %copy-start.21 = (f32[16,8,64]{2,0,1:T(8,128)S(1)}, f32[16,8,64]{2,0,1:T(8,128)}, u32[]{:S(2)}) copy-start(f32[16,8,64]{2,0,1:T(8,128)} %get-tuple-element.221) | copy-start | bytes 98308
  387.7 88.9 %all-reduce.2.cloned.1.call-start = ((), (), s32[]{:S(2)}) async-start(), calls=%async_computation.2 | async-start | bytes 524288 | tf_op jit(solution)/shard_map/psum | solution.py:262
  (175 other events, 538.2 us)
Sparse Core Ops, SparseCore 0:
  20.3 50.0 all-gather.2
  387.9 20.9 reduce-scatter.3
  423.9 52.6 all-reduce.1
where the time goes:
time: 499 us; the launch traced here: 491 us
  local copies, waits for them, and re-layouts  179 us (36%)
  loops' own time  89.8 us (18%)
  other arithmetic  79.8 us (16%)
  waiting for transfers between devices  70.7 us (14%)
  blocking collectives  45.5 us (9%)
  between operations  16 us (3%)
  matrix products  10.6 us (2%)
    psum x1, waiting for transfers between devices, local(): summed = lax.psum(weighted_sum, 'freq')  50.8 us
    another operation x1, loops' own time, gradient_of(): lax.scan(gradient_direction_step, jnp.zeros((), jnp.float32), jnp.arange(...  48.9 us
    another operation x1, loops' own time, residual_of(): lax.scan(residual_direction_step, jnp.zeros(band_vis.shape, jnp.float32),...  40.9 us
    all_gather x1, blocking collectives, local(): all_gains = lax.all_gather(own_gains, 'stn', axis=2, tiled=True)  36.1 us
    mul x32, local copies, waits for them, and re-layouts, complex_mul(): lhs_value[0] * rhs_value[0] - lhs_value[1] * rhs_value[1]  26.2 us
    slice x32, local copies, waits for them, and re-layouts, coherence(): far_imag = lax.dynamic_slice_in_dim(all_table[1], offset, block_span, 1)  25.2 us
    dynamic_slice x32, local copies, waits for them, and re-layouts, coherence(): weight_block = lax.dynamic_slice_in_dim(weights, offset, block_span, 1)  24.3 us
    dynamic_update_slice x16, local copies, waits for them, and re-layouts, gradient_of(): lax.scan(gradient_direction_step, jnp.zeros((), jnp.float32), jnp.arange(...  22.4 us
  transfers between devices with their start and end apart: 3, of which 2 were waited for; matrix products, arithmetic and copies ran while one was open for 5% of the time, Pallas kernels for 0%

commit v1 on v0

v1 whole, which is shorter than its diff:
```python
import functools

import jax
import jax.numpy as jnp
import numpy as np
from jax import lax
from jax.experimental import pallas as pl
from jax.experimental.pallas import tpu as pltpu
from jax.sharding import PartitionSpec as P

DIRS = 16
LANES = 128
PENALTY = 40.0
STEP_SIZE = 0.5
MESH = pl.DeviceIdType.MESH
F32 = jnp.float32
BF16 = jnp.bfloat16


def turn_series(count):
    square = np.linspace(0.0, 0.25, 4001)
    root = np.sqrt(square)
    cosine = np.cos(2 * np.pi * root)
    sine = -2 * np.pi * np.sinc(2 * root)
    fits = []
    for target in (cosine, sine):
        fit = np.polynomial.chebyshev.Chebyshev.fit(square, target, count - 1, domain=[0.0, 0.25])
        fits.append([float(c) for c in fit.convert(kind=np.polynomial.Polynomial).coef])
    return fits


COS_SERIES, SIN_SERIES = turn_series(7)


def basis_rows(band_count):
    centre = (2.0 * np.arange(band_count) + 1.0) / band_count - 1.0
    return np.stack(
        [
            np.ones_like(centre),
            centre,
            0.5 * (3.0 * centre**2 - 1.0),
            0.5 * (5.0 * centre**3 - 3.0 * centre),
        ],
        axis=1,
    )


def horner(series, value):
    total = value * series[-1] + series[-2]
    for coefficient in series[-3::-1]:
        total = total * value + coefficient
    return total


def phasor(turns):
    part = turns - jnp.floor(turns + 0.5)
    square = part * part
    return horner(COS_SERIES, square).astype(BF16), (horner(SIN_SERIES, square) * part).astype(BF16)


def packed(value):
    half = value.shape[0] // 2
    rows, cols = half * value.shape[1], value.shape[2]
    return jnp.concatenate([value[:half].reshape(rows, cols), value[half:].reshape(rows, cols)], 1)


def kernel(
    bands,
    blocks,
    vis_ref,
    mask_ref,
    stations_ref,
    dirs_ref,
    flux_ref,
    pol_ref,
    index_ref,
    clusters_ref,
    gains_ref,
    duals_ref,
    cons_ref,
    jones_out,
    duals_out,
    cons_out,
    near_all,
    vis_send,
    vis_recv,
    grad_send,
    grad_recv,
    norm_recv,
    sums_all,
    oh_rank,
    sky_lhs,
    sky_rows,
    sky_cols,
    jones_cols,
    jones_rows,
    place_rows,
    right,
    terms,
    wide,
    mask_sum,
    grads,
    near_ssem,
    near_rsem,
    vis_ssem,
    vis_rsem,
    grad_ssem,
    grad_rsem,
    norm_ssem,
    norm_rsem,
    sums_ssem,
    sums_rsem,
):
    my_band = lax.axis_index("freq")
    my_block = lax.axis_index("stn")
    rows = gains_ref.shape[2]
    total = vis_ref.shape[2]
    comps = clusters_ref.shape[1]
    span = comps // DIRS

    barrier = pltpu.get_barrier_semaphore()
    stn_peers = [lax.rem(my_block + d, blocks) for d in range(1, blocks)]
    freq_peers = [lax.rem(my_band + d, bands) for d in range(1, bands)]
    for peer in stn_peers:
        pl.semaphore_signal(barrier, inc=1, device_id=(my_band, peer), device_id_type=MESH)
    for peer in freq_peers:
        pl.semaphore_signal(barrier, inc=1, device_id=(peer, my_block), device_id_type=MESH)

    def to_blocks(source_of, target, ssem, rsem):
        copies = []
        for at, peer in enumerate(stn_peers):
            copy = pltpu.make_async_remote_copy(
                src_ref=source_of(peer),
                dst_ref=target.at[my_block],
                send_sem=ssem.at[at],
                recv_sem=rsem.at[at],
                device_id=(my_band, peer),
                device_id_type=MESH,
            )
            copy.start()
            copies.append(copy)
        return copies

    gains = gains_ref[...]
    near_all[my_block, 0 : 8 * DIRS] = gains.reshape(8 * DIRS, rows)
    near_all[my_block, 8 * DIRS : 8 * DIRS + 3] = stations_ref[...]
    pl.semaphore_wait(barrier, blocks - 1 + bands - 1)
    near_copies = to_blocks(lambda peer: near_all.at[my_block], near_all, near_ssem, near_rsem)

    mask = mask_ref[...].astype(F32)
    for pair in range(5):
        if pair < 4:
            first, second = vis_ref[2 * pair] * mask, vis_ref[2 * pair + 1] * mask
        else:
            first = second = mask
        both = jnp.concatenate([first, second], 0)
        turned = both.T
        for block in range(blocks):
            vis_send[block, pair] = turned[block * rows : (block + 1) * rows]
        if pair < 4:
            wide[2 * pair] = first
            wide[2 * pair + 1] = second
        else:
            mask_sum[...] = first
    vis_copies = to_blocks(lambda peer: vis_send.at[peer], vis_recv, vis_ssem, vis_rsem)
    vis_recv[my_block] = vis_send[my_block]

    clusters = clusters_ref[...]
    member = (lax.broadcasted_iota(jnp.int32, (DIRS, comps), 0) == clusters).astype(F32)
    chunks = comps // LANES
    stacked = jnp.concatenate([member[:, c * LANES : (c + 1) * LANES] for c in range(chunks)], 0)
    before = (
        lax.broadcasted_iota(jnp.int32, (LANES, LANES), 0)
        < lax.broadcasted_iota(jnp.int32, (LANES, LANES), 1)
    ).astype(BF16)
    prefix = jnp.dot(stacked.astype(BF16), before, preferred_element_type=F32)
    running = jnp.zeros((DIRS, 1), F32)
    rank_iota = lax.broadcasted_iota(jnp.int32, (LANES, LANES), 0).astype(F32)
    for c in range(chunks):
        own = stacked[c * DIRS : (c + 1) * DIRS]
        rank = jnp.sum(own * (prefix[c * DIRS : (c + 1) * DIRS] + running), 0, keepdims=True)
        oh_rank[:, c * LANES : (c + 1) * LANES] = (rank_iota == rank).astype(F32)
        running = running + jnp.sum(own, 1, keepdims=True)
    values = jnp.concatenate(
        [
            dirs_ref[...],
            flux_ref[...],
            pol_ref[...],
            index_ref[...],
            jnp.zeros((2, comps), F32),
        ],
        0,
    )
    for k in range(DIRS):
        sky_lhs[8 * k : 8 * k + 8] = member[k : k + 1] * values
    sky = lax.dot_general(
        sky_lhs[...],
        oh_rank[...],
        (((1,), (1,)), ((), ())),
        precision=lax.Precision.HIGHEST,
        preferred_element_type=F32,
    )
    sky_rows[...] = sky.reshape(DIRS, 8, LANES)
    sky_turned = sky.T
    for k in range(DIRS):
        sky_cols[k] = sky_turned[:, 8 * k : 8 * k + 8]
        jones_cols[k] = gains[:, k, :].T
    zero_rows = jnp.zeros((LANES - span, 2 * total), BF16)
    right[span:LANES] = zero_rows
    right[LANES + span :] = zero_rows
    band_number = my_band.astype(F32)
    ratio = 0.5 + 3.0 * (band_number + 0.5) / bands
    log_ratio = jnp.log(jnp.full((8, LANES), ratio, F32))[0:1]
    own_place = stations_ref[...].T

    for copy in near_copies:
        copy.wait()
    for block in range(blocks):
        cut = slice(block * rows, (block + 1) * rows)
        jones_rows[:, :, cut] = near_all[block, 0 : 8 * DIRS].reshape(8, DIRS, rows)
        place_rows[0:3, cut] = near_all[block, 8 * DIRS : 8 * DIRS + 3]

    def geometry(l_value, m_value, places):
        n_value = jnp.sqrt(1.0 - l_value * l_value - m_value * m_value) - 1.0
        return ratio * (l_value * places[0] + m_value * places[1] + n_value * places[2])

    @pl.loop(0, DIRS)
    def build_terms(k):
        row = sky_rows[k]
        factor = jnp.exp(row[5:6] * log_ratio)
        w_xx = (row[2:3] + row[3:4]) * factor
        w_xy = row[4:5] * factor
        w_yy = (row[2:3] - row[3:4]) * factor
        turns = geometry(row[0:1], row[1:2], [own_place[:, a : a + 1] for a in range(3)])
        own_r, own_i = (value.astype(F32) for value in phasor(turns))
        jones = jones_cols[k]
        weight = ((w_xx, w_xy), (w_xy, w_yy))
        left = []
        for i in range(2):
            j0r, j0i, j1r, j1i = (jones[:, 4 * i + a : 4 * i + a + 1] for a in range(4))
            for j in range(2):
                e_r = j0r * weight[0][j] + j1r * weight[1][j]
                e_i = j0i * weight[0][j] + j1i * weight[1][j]
                left.append(
                    jnp.concatenate(
                        [
                            (own_r * e_r - own_i * e_i).astype(BF16),
                            (own_r * e_i + own_i * e_r).astype(BF16),
                        ],
                        1,
                    )
                )
        col = sky_cols[k][0:span]
        places = [place_rows[a : a + 1, :] for a in range(3)]
        far_r, far_i = phasor(geometry(col[:, 0:1], col[:, 1:2], places))
        right[0:span, 0:total] = far_r
        right[0:span, total:] = -far_i
        right[LANES : LANES + span, 0:total] = far_i
        right[LANES : LANES + span, total:] = far_r
        terms[k] = jnp.dot(
            jnp.concatenate(left, 0), right[...], preferred_element_type=F32
        )

    for copy in vis_copies:
        copy.wait()
    for i in range(2):
        for j in range(2):
            for part in range(2):
                lanes = slice(part * rows, (part + 1) * rows)
                other = jnp.concatenate(
                    [vis_recv[block, 2 * j + i, :, lanes] for block in range(blocks)], 1
                )
                at = 2 * (2 * i + j) + part
                wide[at] = wide[at] + other if part == 0 else wide[at] - other
    mask_sum[...] += jnp.concatenate([vis_recv[block, 4, :, 0:rows] for block in range(blocks)], 1)

    def term_parts(k, row_at):
        out = []
        for entry in range(4):
            cut = pl.ds(pl.multiple_of(entry * rows + row_at * 8, 8), 8)
            out.append((terms[k, cut, 0:total], terms[k, cut, total:]))
        return out

    @pl.loop(0, rows // 8)
    def subtract_model(row_at):
        def add_direction(k, sums):
            t = term_parts(k, row_at)
            sums = list(sums)
            for el in range(2):
                for j in range(2):
                    j_r = jones_rows[2 * (2 * el + j), pl.ds(k, 1), :]
                    j_i = jones_rows[2 * (2 * el + j) + 1, pl.ds(k, 1), :]
                    for i in range(2):
                        t_r, t_i = t[2 * i + j]
                        at = 2 * (2 * i + el)
                        sums[at] = sums[at] + (t_r * j_r + t_i * j_i)
                        sums[at + 1] = sums[at + 1] + (t_i * j_r - t_r * j_i)
            return tuple(sums)

        sums = lax.fori_loop(
            0, DIRS, add_direction, tuple(jnp.zeros((8, total), F32) for _ in range(8))
        )
        cut = pl.ds(pl.multiple_of(row_at * 8, 8), 8)
        both = mask_sum[cut]
        for at in range(8):
            wide[at, cut] = wide[at, cut] - both * sums[at]

    @pl.loop(0, DIRS)
    def gradient(k):
        def add_rows(row_at, sums):
            t = term_parts(k, row_at)
            cut = pl.ds(pl.multiple_of(row_at * 8, 8), 8)
            sums = list(sums)
            for m in range(2):
                for i in range(2):
                    w_r = wide[2 * (2 * m + i), cut]
                    w_i = wide[2 * (2 * m + i) + 1, cut]
                    for j in range(2):
                        t_r, t_i = t[2 * m + j]
                        at = 2 * (2 * i + j)
                        sums[at] = sums[at] + (w_r * t_r + w_i * t_i)
                        sums[at + 1] = sums[at + 1] + (w_r * t_i - w_i * t_r)
            return tuple(sums)

        sums = lax.fori_loop(
            0, rows // 8, add_rows, tuple(jnp.zeros((8, total), F32) for _ in range(8))
        )
        for at in range(8):
            grads[at, pl.ds(k, 1), :] = -jnp.sum(sums[at], 0, keepdims=True)

    for block in range(blocks):
        grad_send[block] = packed(grads[:, :, block * rows : (block + 1) * rows])
    grad_copies = to_blocks(lambda peer: grad_send.at[peer], grad_recv, grad_ssem, grad_rsem)
    centre = (2.0 * band_number + 1.0) / bands - 1.0
    basis = (
        1.0,
        centre,
        0.5 * (3.0 * centre * centre - 1.0),
        0.5 * (5.0 * centre * centre * centre - 3.0 * centre),
    )
    own_jones = packed(gains)
    own_duals = packed(duals_ref[...])
    poly = packed(cons_ref[0])
    for i in range(1, 4):
        poly = poly + basis[i] * packed(cons_ref[i])
    drive = PENALTY / 2.0 * (own_jones - poly + own_duals) + grad_send[my_block]
    for copy in grad_copies:
        copy.wait()
    for peer in stn_peers:
        drive = drive + grad_recv[peer]
    squares = jnp.sum((drive * drive).reshape(-1, 8, 2 * rows), 0)
    norm_recv[my_block] = squares
    norm_copies = to_blocks(lambda peer: norm_recv.at[my_block], norm_recv, norm_ssem, norm_rsem)
    for copy in norm_copies:
        copy.wait()
    squares = norm_recv[0]
    for block in range(1, blocks):
        squares = squares + norm_recv[block]
    mean = jnp.sum(jnp.sum(squares, 0, keepdims=True), 1, keepdims=True) / (8 * DIRS * total)
    step = STEP_SIZE / jnp.sqrt(mean + 1e-06)
    jones_next = own_jones - step * drive
    base = jones_next + own_duals
    sums_all[my_band] = base
    copies = []
    for at, peer in enumerate(freq_peers):
        copy = pltpu.make_async_remote_copy(
            src_ref=sums_all.at[my_band],
            dst_ref=sums_all.at[my_band],
            send_sem=sums_ssem.at[at],
            recv_sem=sums_rsem.at[at],
            device_id=(peer, my_block),
            device_id_type=MESH,
        )
        copy.start()
        copies.append(copy)

    def unpacked(value):
        return [
            value[:, part * rows : (part + 1) * rows].reshape(4, DIRS, rows) for part in range(2)
        ]

    for part, piece in enumerate(unpacked(jones_next)):
        jones_out[4 * part : 4 * part + 4] = piece
    for copy in copies:
        copy.wait()
    table = basis_rows(bands)
    solve = np.linalg.solve(table.T @ table, table.T)
    fitted = None
    for i in range(4):
        value = float(solve[i, 0]) * sums_all[0]
        for band in range(1, bands):
            value = value + float(solve[i, band]) * sums_all[band]
        for part, piece in enumerate(unpacked(value)):
            cons_out[i, 4 * part : 4 * part + 4] = piece
        fitted = value if i == 0 else fitted + basis[i] * value
    for part, piece in enumerate(unpacked(base - fitted)):
        duals_out[4 * part : 4 * part + 4] = piece


def local(
    visibilities,
    flag_mask,
    stations,
    directions,
    intensity,
    polarized,
    spectral,
    clusters,
    jones_gains,
    scaled_duals,
    consensus,
):
    bands = lax.axis_size("freq")
    blocks = lax.axis_size("stn")
    rows, total = flag_mask.shape
    comps = clusters.shape[0]
    vmem = pl.BlockSpec(memory_space=pltpu.VMEM)
    block_sem = pltpu.SemaphoreType.DMA((blocks - 1,))
    outs = pl.pallas_call(
        functools.partial(kernel, bands, blocks),
        out_shape=(
            jax.ShapeDtypeStruct((8, DIRS, rows), F32),
            jax.ShapeDtypeStruct((8, DIRS, rows), F32),
            jax.ShapeDtypeStruct((4, 8, DIRS, rows), F32),
        ),
        in_specs=[vmem] * 11,
        out_specs=(vmem, vmem, vmem),
        scratch_shapes=[
            pltpu.VMEM((blocks, 8 * DIRS + 8, rows), F32),
            pltpu.VMEM((blocks, 5, rows, 2 * rows), F32),
            pltpu.VMEM((blocks, 5, rows, 2 * rows), F32),
            pltpu.VMEM((blocks, 4 * DIRS, 2 * rows), F32),
            pltpu.VMEM((blocks, 4 * DIRS, 2 * rows), F32),
            pltpu.VMEM((blocks, 8, 2 * rows), F32),
            pltpu.VMEM((bands, 4 * DIRS, 2 * rows), F32),
            pltpu.VMEM((LANES, comps), F32),
            pltpu.VMEM((8 * DIRS, comps), F32),
            pltpu.VMEM((DIRS, 8, LANES), F32),
            pltpu.VMEM((DIRS, LANES, 8), F32),
            pltpu.VMEM((DIRS, rows, 8), F32),
            pltpu.VMEM((8, DIRS, total), F32),
            pltpu.VMEM((8, total), F32),
            pltpu.VMEM((2 * LANES, 2 * total), BF16),
            pltpu.VMEM((DIRS, 4 * rows, 2 * total), F32),
            pltpu.VMEM((8, rows, total), F32),
            pltpu.VMEM((rows, total), F32),
            pltpu.VMEM((8, DIRS, total), F32),
        ]
        + [block_sem] * 8
        + [pltpu.SemaphoreType.DMA((bands - 1,))] * 2,
        compiler_params=pltpu.CompilerParams(
            collective_id=0, has_side_effects=True, vmem_limit_bytes=58 * 1024 * 1024
        ),
    )(
        visibilities[0],
        flag_mask,
        stations,
        directions,
        intensity[None],
        polarized,
        spectral[None],
        clusters[None],
        jones_gains[0],
        scaled_duals[0],
        consensus,
    )
    return (outs[0][None], outs[1][None], outs[2])


def solution(mesh):
    placed = (
        P("freq", None, "stn", None),
        P("stn", None),
        P(None, "stn"),
        P(),
        P(),
        P(),
        P(),
        P(),
        P("freq", None, None, "stn"),
        P("freq", None, None, "stn"),
        P(None, None, None, "stn"),
    )
    return jax.shard_map(
        local,
        mesh=mesh,
        in_specs=placed,
        out_specs=(
            P("freq", None, None, "stn"),
            P("freq", None, None, "stn"),
            P(None, None, None, "stn"),
        ),
        check_vma=False,
    )
```

time: 499 us -> 57.1 us (0.11); the launches traced: 491 us -> 56.8 us
  local copies, waits for them, and re-layouts: 179 us -> 6.3 us
  loops' own time: 89.8 us -> 0 us
  other arithmetic: 79.8 us -> 0 us
  waiting for transfers between devices: 70.7 us -> 0 us
  Pallas kernels: 0 us -> 49.9 us
  blocking collectives: 45.5 us -> 0 us
  between operations: 16 us -> 0.66 us
  matrix products: 10.6 us -> 0 us
    another operation x2 -> x0, loops' own time: 89.8 us -> none  [the longest x1 48.9 us: gradient_of(): lax.scan(gradient_direction_step, jnp.zeros((), jnp.float32), jnp.arange(...]
    psum x1 -> x0, waiting for transfers between devices: 50.8 us -> none  [local(): summed = lax.psum(weighted_sum, 'freq')]
    pallas_call x0 -> x1, Pallas kernels: none -> 49.9 us  [local(): pl.pallas_call(functools.partial(kernel, bands, blocks), out_shape=(jax.S...]
    dynamic_slice x96 -> x0, local copies, waits for them, and re-layouts: 48 us -> none  [the longest x32 24.3 us: coherence(): weight_block = lax.dynamic_slice_in_dim(weights, offset, block_span, 1)]
    slice x82 -> x0, local copies, waits for them, and re-layouts: 41 us -> none  [the longest x32 25.2 us: coherence(): far_imag = lax.dynamic_slice_in_dim(all_table[1], offset, block_span, 1)]
    all_gather x1 -> x0, blocking collectives: 36.1 us -> none  [local(): all_gains = lax.all_gather(own_gains, 'stn', axis=2, tiled=True)]
    mul x65 -> x0, local copies, waits for them, and re-layouts: 26.4 us -> none  [the longest x32 26.2 us: complex_mul(): lhs_value[0] * rhs_value[0] - lhs_value[1] * rhs_value[1]]
    gather x6 -> x0, local copies, waits for them, and re-layouts: 22.5 us -> none  [the longest x1 8.39 us: local(): sky_index = spectral[sort_order]]
  transfers between devices with their start and end apart: 3 -> 0, of which waited for: 2 -> 0; matrix products, arithmetic and copies ran while one was open for 5% -> 0% of each run, Pallas kernels for 0% -> 0%
where the time goes in v1:
time: 57.1 us; the launch traced here: 56.8 us
  Pallas kernels  49.9 us (87%)
  local copies, waits for them, and re-layouts  6.3 us (11%)
  between operations  0.66 us (1%)
    pallas_call x1, Pallas kernels, local(): pl.pallas_call(functools.partial(kernel, bands, blocks), out_shape=(jax.S...  49.9 us
    unnamed x9, local copies, waits for them, and re-layouts  3.8 us
    broadcast_in_dim x1, local copies, waits for them, and re-layouts, local(): intensity[None]  1.3 us

profile of v1, /device:TPU:0, one launch (start us, length us, event | category | flops | bytes accessed | tf_op | source)
XLA Modules:
  0.0 56.8 jit_solution(6726574162508667639)
XLA Ops:
  0.6 0.0 copy-start.1
  0.6 1.3 %broadcast_in_dim.15.flux_ref = f32[1,1536]{1,0:T(1,128)} reshape(f32[1536]{0:T(1024)} %param.15) | data formatting | bytes 12288 | tf_op jit(solution)/shard_map/broadcast_in_dim | solution.py:459
  1.9 0.0 copy-done.1
  1.9 0.0 copy-start.2
  1.9 0.6 %broadcast_in_dim.16.index_ref = f32[1,1536]{1,0:T(1,128)} reshape(f32[1536]{0:T(1024)S(1)} %copy-done.1) | data formatting | bytes 12288 | tf_op jit(solution)/shard_map/broadcast_in_dim | solution.py:461
  2.5 0.1 copy-done.2
  2.6 0.6 %broadcast_in_dim.17.clusters_ref = s32[1,1536]{1,0:T(1,128)} reshape(s32[1536]{0:T(1024)S(1)} %copy-done.2) | data formatting | bytes 12288 | tf_op jit(solution)/shard_map/broadcast_in_dim | solution.py:462
  3.2 49.9 %shard_map.130 = (f32[8,16,64]{2,1,0:T(8,128)}, f32[8,16,64]{2,1,0:T(8,128)}, f32[4,8,16,64]{3,2,1,0:T(8,128)}) custom-call(f32[8,64,256]{2,1,0:T(8,128)} %bitcast.5, s32[64,256]{1,0:T(8,128)} %mask_ref.1, f32[3,64]{1,0:T(4,128)} %stations_ref.1, f32[2,1536]{1,0:T(2,128)} %dirs_ref.1, f32[1,1536]{1,0:T(1,128)} %broadcast_in_dim.15.flux_ref, ...), custom_call_target="tpu_custom_call" | custom-call | tf_op jit(solution)/shard_map/pallas_call | solution.py:419
  53.1 0.0 copy-start
  53.1 1.5 %copy.17 = f32[1,8,16,64]{3,2,1,0:T(8,128)} copy(f32[1,8,16,64]{3,2,1,0:T(8,128)} %bitcast.9) | data formatting | bytes 65536
  54.6 1.5 %copy.18 = f32[1,8,16,64]{3,2,1,0:T(8,128)} copy(f32[1,8,16,64]{3,2,1,0:T(8,128)} %bitcast.8) | data formatting | bytes 65536
  56.1 0.0 copy-done
  56.1 0.7 %copy.19 = f32[4,8,16,64]{3,2,1,0:T(8,128)} copy(f32[4,8,16,64]{3,2,1,0:T(8,128)S(1)} %copy-done) | data formatting | bytes 262144
Async XLA Ops:
  0.6 1.3 %copy-start.1 = (f32[1536]{0:T(1024)S(1)}, f32[1536]{0:T(1024)}, u32[]{:S(2)}) copy-start(f32[1536]{0:T(1024)} %param.17) | copy-start | bytes 18436
  1.9 0.7 %copy-start.2 = (s32[1536]{0:T(1024)S(1)}, s32[1536]{0:T(1024)}, u32[]{:S(2)}) copy-start(s32[1536]{0:T(1024)} %param.18) | copy-start | bytes 18436
  53.1 3.0 %copy-start = (f32[4,8,16,64]{3,2,1,0:T(8,128)S(1)}, f32[4,8,16,64]{3,2,1,0:T(8,128)}, u32[]{:S(2)}) copy-start(f32[4,8,16,64]{3,2,1,0:T(8,128)} %get-tuple-element.14) | copy-start | bytes 393220

commit v2 on v1

v2 whole, which is shorter than its diff:
```python
import functools

import jax
import jax.numpy as jnp
import numpy as np
from jax import lax
from jax.experimental import pallas as pl
from jax.experimental.pallas import tpu as pltpu
from jax.sharding import PartitionSpec as P

DIRS = 16
LANES = 128
PENALTY = 40.0
STEP_SIZE = 0.5
MESH = pl.DeviceIdType.MESH
F32 = jnp.float32
BF16 = jnp.bfloat16


def turn_series(count):
    square = np.linspace(0.0, 0.25, 4001)
    root = np.sqrt(square)
    cosine = np.cos(2 * np.pi * root)
    sine = -2 * np.pi * np.sinc(2 * root)
    fits = []
    for target in (cosine, sine):
        fit = np.polynomial.chebyshev.Chebyshev.fit(square, target, count - 1, domain=[0.0, 0.25])
        fits.append([float(c) for c in fit.convert(kind=np.polynomial.Polynomial).coef])
    return fits


COS_SERIES, SIN_SERIES = turn_series(7)


def basis_rows(band_count):
    centre = (2.0 * np.arange(band_count) + 1.0) / band_count - 1.0
    return np.stack(
        [
            np.ones_like(centre),
            centre,
            0.5 * (3.0 * centre**2 - 1.0),
            0.5 * (5.0 * centre**3 - 3.0 * centre),
        ],
        axis=1,
    )


def horner(series, value):
    total = value * series[-1] + series[-2]
    for coefficient in series[-3::-1]:
        total = total * value + coefficient
    return total


def phasor(turns):
    part = turns - jnp.floor(turns + 0.5)
    square = part * part
    return horner(COS_SERIES, square).astype(BF16), (horner(SIN_SERIES, square) * part).astype(BF16)


def packed(value):
    half = value.shape[0] // 2
    rows, cols = half * value.shape[1], value.shape[2]
    return jnp.concatenate([value[:half].reshape(rows, cols), value[half:].reshape(rows, cols)], 1)


def kernel(
    bands,
    blocks,
    vis_ref,
    mask_ref,
    stations_ref,
    dirs_ref,
    flux_ref,
    pol_ref,
    index_ref,
    clusters_ref,
    gains_ref,
    duals_ref,
    cons_ref,
    result,
    near_all,
    vis_send,
    vis_recv,
    base_all,
    drive_all,
    norm_all,
    step_all,
    oh_rank,
    sky_lhs,
    sky_rows,
    sky_cols,
    jones_cols,
    jones_rows,
    place_rows,
    left_even,
    left_odd,
    right_even,
    right_odd,
    coh,
    far_terms,
    wide,
    mask_sum,
    grad_cols,
    near_ssem,
    near_rsem,
    vis_ssem,
    vis_rsem,
    norm_ssem,
    norm_rsem,
    base_ssem,
    base_rsem,
    drive_ssem,
    drive_rsem,
    step_ssem,
    step_rsem,
):
    my_band = lax.axis_index("freq")
    my_block = lax.axis_index("stn")
    rows = gains_ref.shape[2]
    total = vis_ref.shape[2]
    comps = clusters_ref.shape[0]
    span = comps // DIRS

    barrier = pltpu.get_barrier_semaphore()
    stn_peers = [lax.rem(my_block + d, blocks) for d in range(1, blocks)]
    freq_peers = [lax.rem(my_band + d, bands) for d in range(1, bands)]
    for peer in stn_peers:
        pl.semaphore_signal(barrier, inc=1, device_id=(my_band, peer), device_id_type=MESH)
    for peer in freq_peers:
        pl.semaphore_signal(barrier, inc=1, device_id=(peer, my_block), device_id_type=MESH)

    def send(source, target, ssem, rsem, at, device):
        copy = pltpu.make_async_remote_copy(
            src_ref=source,
            dst_ref=target,
            send_sem=ssem.at[at],
            recv_sem=rsem.at[at],
            device_id=device,
            device_id_type=MESH,
        )
        copy.start()
        return copy

    def to_blocks(source_of, target, ssem, rsem):
        return [
            send(source_of(peer), target.at[my_block], ssem, rsem, at, (my_band, peer))
            for at, peer in enumerate(stn_peers)
        ]

    def to_bands(target, ssem, rsem):
        own = target.at[my_band]
        return [
            send(own, own, ssem, rsem, at, (peer, my_block)) for at, peer in enumerate(freq_peers)
        ]

    gains = gains_ref[...]
    near_all[my_block, 0 : 8 * DIRS] = gains.reshape(8 * DIRS, rows)
    near_all[my_block, 8 * DIRS : 8 * DIRS + 3] = stations_ref[...]
    own_jones = packed(gains)
    base_all[my_band] = own_jones + packed(duals_ref[...])

    mask = mask_ref[...].astype(F32)
    for pair in range(5):
        if pair < 4:
            first, second = vis_ref[2 * pair] * mask, vis_ref[2 * pair + 1] * mask
        else:
            first = second = mask
        turned = jnp.concatenate([first, second], 0).T
        for block in range(blocks):
            vis_send[block, pair] = turned[block * rows : (block + 1) * rows]
        if pair < 4:
            wide[2 * pair] = first
            wide[2 * pair + 1] = second
        else:
            mask_sum[...] = first
    pl.semaphore_wait(barrier, blocks - 1 + bands - 1)
    near_copies = to_blocks(lambda peer: near_all.at[my_block], near_all, near_ssem, near_rsem)
    vis_copies = to_blocks(lambda peer: vis_send.at[peer], vis_recv, vis_ssem, vis_rsem)
    base_copies = to_bands(base_all, base_ssem, base_rsem)
    vis_recv[my_block] = vis_send[my_block]

    clusters = clusters_ref[...].reshape(1, comps)
    member = (lax.broadcasted_iota(jnp.int32, (DIRS, comps), 0) == clusters).astype(F32)
    chunks = comps // LANES
    stacked = jnp.concatenate([member[:, c * LANES : (c + 1) * LANES] for c in range(chunks)], 0)
    before = (
        lax.broadcasted_iota(jnp.int32, (LANES, LANES), 0)
        < lax.broadcasted_iota(jnp.int32, (LANES, LANES), 1)
    ).astype(BF16)
    prefix = jnp.dot(stacked.astype(BF16), before, preferred_element_type=F32)
    running = jnp.zeros((DIRS, 1), F32)
    rank_iota = lax.broadcasted_iota(jnp.int32, (LANES, LANES), 0).astype(F32)
    for c in range(chunks):
        own = stacked[c * DIRS : (c + 1) * DIRS]
        rank = jnp.sum(own * (prefix[c * DIRS : (c + 1) * DIRS] + running), 0, keepdims=True)
        oh_rank[:, c * LANES : (c + 1) * LANES] = (rank_iota == rank).astype(BF16)
        running = running + jnp.sum(own, 1, keepdims=True)
    values = jnp.concatenate(
        [
            dirs_ref[...],
            flux_ref[...].reshape(1, comps),
            pol_ref[...],
            index_ref[...].reshape(1, comps),
            jnp.zeros((2, comps), F32),
        ],
        0,
    )
    high = values.astype(BF16).astype(F32)
    middle = (values - high).astype(BF16).astype(F32)
    low = values - high - middle
    parts = jnp.concatenate([high, middle, low, jnp.zeros_like(low)], 0)
    for k in range(DIRS):
        sky_lhs[32 * k : 32 * k + 32] = (member[k : k + 1] * parts).astype(BF16)
    sky = lax.dot_general(
        sky_lhs[...], oh_rank[...], (((1,), (1,)), ((), ())), preferred_element_type=F32
    ).reshape(DIRS, 4, 8, LANES)
    sky = (sky[:, 2] + sky[:, 1]) + sky[:, 0]
    sky_rows[...] = sky
    sky_turned = sky.reshape(DIRS * 8, LANES).T
    for k in range(DIRS):
        sky_cols[k] = sky_turned[:, 8 * k : 8 * k + 8]
        jones_cols[k] = gains[:, k, :].T
    zero_rows = jnp.zeros((LANES - span, 2 * total), BF16)
    for right in (right_even, right_odd):
        right[span:LANES] = zero_rows
        right[LANES + span :] = zero_rows
    band_number = my_band.astype(F32)
    ratio = 0.5 + 3.0 * (band_number + 0.5) / bands
    log_ratio = jnp.log(jnp.full((8, LANES), ratio, F32))[0:1]
    own_place = stations_ref[...].T

    for copy in near_copies:
        copy.wait()
    for block in range(blocks):
        cut = slice(block * rows, (block + 1) * rows)
        jones_rows[:, :, cut] = near_all[block, 0 : 8 * DIRS].reshape(8, DIRS, rows)
        place_rows[0:3, cut] = near_all[block, 8 * DIRS : 8 * DIRS + 3]

    def geometry(l_value, m_value, places):
        n_value = jnp.sqrt(1.0 - l_value * l_value - m_value * m_value) - 1.0
        return ratio * (l_value * places[0] + m_value * places[1] + n_value * places[2])

    def build(k, left, right):
        row = sky_rows[k]
        factor = jnp.exp(row[5:6] * log_ratio)
        weights = (
            (row[2:3] + row[3:4]) * factor,
            row[4:5] * factor,
            (row[2:3] - row[3:4]) * factor,
        )
        turns = geometry(row[0:1], row[1:2], [own_place[:, a : a + 1] for a in range(3)])
        own_r, own_i = (value.astype(F32) for value in phasor(turns))
        for at, weight in enumerate(weights):
            left[at * rows : (at + 1) * rows, 0:LANES] = (own_r * weight).astype(BF16)
            left[at * rows : (at + 1) * rows, LANES:] = (own_i * weight).astype(BF16)
        col = sky_cols[k][0:span]
        places = [place_rows[a : a + 1, :] for a in range(3)]
        far_r, far_i = phasor(geometry(col[:, 0:1], col[:, 1:2], places))
        right[0:span, 0:total] = far_r
        right[0:span, total:] = -far_i
        right[LANES : LANES + span, 0:total] = far_i
        right[LANES : LANES + span, total:] = far_r

    def multiply(k, left, right):
        coh[k] = jnp.dot(left[...], right[...], preferred_element_type=F32)

    build(0, left_even, right_even)

    @pl.loop(0, DIRS // 2)
    def coherencies(at):
        build(2 * at + 1, left_odd, right_odd)
        multiply(2 * at, left_even, right_even)
        build(jnp.minimum(2 * at + 2, DIRS - 1), left_even, right_even)
        multiply(2 * at + 1, left_odd, right_odd)

    for copy in vis_copies:
        copy.wait()
    for i in range(2):
        for j in range(2):
            for part in range(2):
                lanes = slice(part * rows, (part + 1) * rows)
                other = jnp.concatenate(
                    [vis_recv[block, 2 * j + i, :, lanes] for block in range(blocks)], 1
                )
                at = 2 * (2 * i + j) + part
                wide[at] = wide[at] + other if part == 0 else wide[at] - other
    mask_sum[...] += jnp.concatenate([vis_recv[block, 4, :, 0:rows] for block in range(blocks)], 1)
    lane = lax.broadcasted_iota(jnp.int32, (8, 8 * DIRS), 1)

    @pl.loop(0, rows // 8)
    def gradient(row_at):
        cut = pl.ds(pl.multiple_of(row_at * 8, 8), 8)

        def add_model(k, sums):
            entries = []
            for at in range(3):
                rows_at = pl.ds(pl.multiple_of(at * rows + row_at * 8, 8), 8)
                entries.append((coh[k, rows_at, 0:total], coh[k, rows_at, total:]))
            matrix = ((entries[0], entries[1]), (entries[1], entries[2]))
            near = jones_cols[k, cut, :]
            sums = list(sums)
            for el in range(2):
                far = [
                    tuple(jones_rows[4 * el + 2 * n + a, pl.ds(k, 1), :] for a in range(2))
                    for n in range(2)
                ]
                for m in range(2):
                    (a_r, a_i), (b_r, b_i) = matrix[m]
                    (c_r, c_i), (d_r, d_i) = far
                    y_r = (a_r * c_r + a_i * c_i) + (b_r * d_r + b_i * d_i)
                    y_i = (a_i * c_r - a_r * c_i) + (b_i * d_r - b_r * d_i)
                    far_terms[k, 4 * m + 2 * el] = y_r
                    far_terms[k, 4 * m + 2 * el + 1] = y_i
                    for i in range(2):
                        p_r = near[:, 4 * i + 2 * m : 4 * i + 2 * m + 1]
                        p_i = near[:, 4 * i + 2 * m + 1 : 4 * i + 2 * m + 2]
                        at = 4 * i + 2 * el
                        sums[at] = sums[at] + (p_r * y_r - p_i * y_i)
                        sums[at + 1] = sums[at + 1] + (p_r * y_i + p_i * y_r)
            return tuple(sums)

        sums = lax.fori_loop(
            0, DIRS, add_model, tuple(jnp.zeros((8, total), F32) for _ in range(8)), unroll=2
        )
        both = mask_sum[cut]
        w = [wide[at, cut] - both * sums[at] for at in range(8)]

        def add_gradient(k, columns):
            y = [far_terms[k, at] for at in range(8)]
            for i in range(2):
                for j in range(2):
                    real = imag = None
                    for m in range(2):
                        w_r, w_i = w[4 * i + 2 * m], w[4 * i + 2 * m + 1]
                        y_r, y_i = y[4 * j + 2 * m], y[4 * j + 2 * m + 1]
                        one, two = w_r * y_r + w_i * y_i, w_i * y_r - w_r * y_i
                        real, imag = (one, two) if m == 0 else (real + one, imag + two)
                    for part, member_sum in enumerate((real, imag)):
                        place = (4 * i + 2 * j + part) * DIRS + k
                        summed = jnp.sum(member_sum, 1, keepdims=True)
                        columns = jnp.where(lane == place, summed, columns)
            return columns

        grad_cols[cut] = lax.fori_loop(
            0, DIRS, add_gradient, jnp.zeros((8, 8 * DIRS), F32), unroll=4
        )

    centre = (2.0 * band_number + 1.0) / bands - 1.0
    basis = (
        1.0,
        centre,
        0.5 * (3.0 * centre * centre - 1.0),
        0.5 * (5.0 * centre * centre * centre - 3.0 * centre),
    )
    poly = packed(cons_ref[0])
    for i in range(1, 4):
        poly = poly + basis[i] * packed(cons_ref[i])
    base = base_all[my_band]
    turned = grad_cols[...].T
    grads = jnp.concatenate([turned[0 : 4 * DIRS], turned[4 * DIRS :]], 1)
    drive = PENALTY / 2.0 * (base - poly) - grads
    drive_all[my_band] = drive
    norm_all[my_block] = jnp.sum((drive * drive).reshape(-1, 8, 2 * rows), 0)
    norm_copies = to_blocks(lambda peer: norm_all.at[my_block], norm_all, norm_ssem, norm_rsem)
    drive_copies = to_bands(drive_all, drive_ssem, drive_rsem)
    for copy in norm_copies:
        copy.wait()
    squares = norm_all[0]
    for block in range(1, blocks):
        squares = squares + norm_all[block]
    mean = jnp.sum(jnp.sum(squares, 0, keepdims=True), 1, keepdims=True) / (8 * DIRS * total)
    step_all[my_band] = jnp.broadcast_to(STEP_SIZE / jnp.sqrt(mean + 1e-06), (8, 2 * rows))
    step_copies = to_bands(step_all, step_ssem, step_rsem)
    result[0] = own_jones - step_all[my_band, 0:1] * drive
    for copy in base_copies + drive_copies + step_copies:
        copy.wait()
    sums = [
        base_all[band] - step_all[band, 0:1] * drive_all[band] for band in range(bands)
    ]
    table = basis_rows(bands)
    solve = np.linalg.solve(table.T @ table, table.T)
    fitted = None
    for i in range(4):
        value = float(solve[i, 0]) * sums[0]
        for band in range(1, bands):
            value = value + float(solve[i, band]) * sums[band]
        result[2 + i] = value
        fitted = value if i == 0 else fitted + basis[i] * value
    result[1] = base - step_all[my_band, 0:1] * drive - fitted


def spread(result, jones_out, duals_out, cons_out):
    rows = jones_out.shape[2]
    for part in range(2):
        lanes = slice(part * rows, (part + 1) * rows)
        cut = slice(4 * part, 4 * part + 4)
        jones_out[cut] = result[0, :, lanes].reshape(4, DIRS, rows)
        duals_out[cut] = result[1, :, lanes].reshape(4, DIRS, rows)
        for i in range(4):
            cons_out[i, cut] = result[2 + i, :, lanes].reshape(4, DIRS, rows)


def local(
    visibilities,
    flag_mask,
    stations,
    directions,
    intensity,
    polarized,
    spectral,
    clusters,
    jones_gains,
    scaled_duals,
    consensus,
):
    bands = lax.axis_size("freq")
    blocks = lax.axis_size("stn")
    rows, total = flag_mask.shape
    comps = clusters.shape[0]
    vmem = pl.BlockSpec(memory_space=pltpu.VMEM)
    block_sem = pltpu.SemaphoreType.DMA((blocks - 1,))
    band_sem = pltpu.SemaphoreType.DMA((bands - 1,))
    result = pl.pallas_call(
        functools.partial(kernel, bands, blocks),
        out_shape=jax.ShapeDtypeStruct((6, 4 * DIRS, 2 * rows), F32),
        in_specs=[vmem] * 11,
        out_specs=vmem,
        scratch_shapes=[
            pltpu.VMEM((blocks, 8 * DIRS + 8, rows), F32),
            pltpu.VMEM((blocks, 5, rows, 2 * rows), F32),
            pltpu.VMEM((blocks, 5, rows, 2 * rows), F32),
            pltpu.VMEM((bands, 4 * DIRS, 2 * rows), F32),
            pltpu.VMEM((bands, 4 * DIRS, 2 * rows), F32),
            pltpu.VMEM((blocks, 8, 2 * rows), F32),
            pltpu.VMEM((bands, 8, 2 * rows), F32),
            pltpu.VMEM((LANES, comps), BF16),
            pltpu.VMEM((32 * DIRS, comps), BF16),
            pltpu.VMEM((DIRS, 8, LANES), F32),
            pltpu.VMEM((DIRS, LANES, 8), F32),
            pltpu.VMEM((DIRS, rows, 8), F32),
            pltpu.VMEM((8, DIRS, total), F32),
            pltpu.VMEM((8, total), F32),
            pltpu.VMEM((3 * rows, 2 * LANES), BF16),
            pltpu.VMEM((3 * rows, 2 * LANES), BF16),
            pltpu.VMEM((2 * LANES, 2 * total), BF16),
            pltpu.VMEM((2 * LANES, 2 * total), BF16),
            pltpu.VMEM((DIRS, 3 * rows, 2 * total), F32),
            pltpu.VMEM((DIRS, 8, 8, total), F32),
            pltpu.VMEM((8, rows, total), F32),
            pltpu.VMEM((rows, total), F32),
            pltpu.VMEM((rows, 8 * DIRS), F32),
        ]
        + [block_sem] * 6
        + [band_sem] * 6,
        compiler_params=pltpu.CompilerParams(
            collective_id=0, has_side_effects=True, vmem_limit_bytes=58 * 1024 * 1024
        ),
    )(
        visibilities[0],
        flag_mask,
        stations,
        directions,
        intensity,
        polarized,
        spectral,
        clusters,
        jones_gains[0],
        scaled_duals[0],
        consensus,
    )
    outs = pl.pallas_call(
        spread,
        out_shape=(
            jax.ShapeDtypeStruct((8, DIRS, rows), F32),
            jax.ShapeDtypeStruct((8, DIRS, rows), F32),
            jax.ShapeDtypeStruct((4, 8, DIRS, rows), F32),
        ),
        in_specs=[vmem],
        out_specs=(vmem, vmem, vmem),
    )(result)
    return (outs[0][None], outs[1][None], outs[2])


def solution(mesh):
    placed = (
        P("freq", None, "stn", None),
        P("stn", None),
        P(None, "stn"),
        P(),
        P(),
        P(),
        P(),
        P(),
        P("freq", None, None, "stn"),
        P("freq", None, None, "stn"),
        P(None, None, None, "stn"),
    )
    return jax.shard_map(
        local,
        mesh=mesh,
        in_specs=placed,
        out_specs=(
            P("freq", None, None, "stn"),
            P("freq", None, None, "stn"),
            P(None, None, None, "stn"),
        ),
        check_vma=False,
    )
```

time: 57.1 us -> 51.3 us (0.90)
  local copies, waits for them, and re-layouts: 6.3 us -> 0 us
  Pallas kernels: 49.9 us -> 50.5 us
    unnamed x9 -> x0, local copies, waits for them, and re-layouts: 3.8 us -> none
    broadcast_in_dim x3 -> x0, local copies, waits for them, and re-layouts: 2.5 us -> none  [the longest x1 1.3 us: local(): intensity[None]]
    pallas_call x1 -> x2, Pallas kernels: 49.9 us -> 50.5 us  [the longest x1 48.7 us: local(): pl.pallas_call(functools.partial(kernel, bands, blocks), out_shape=jax.Sh...]
where the time goes in v2:
time: 51.3 us; the launch traced here: 51.1 us
  Pallas kernels  50.5 us (98%)
  between operations  0.64 us (1%)
    pallas_call x1, Pallas kernels, local(): pl.pallas_call(functools.partial(kernel, bands, blocks), out_shape=jax.Sh...  48.7 us
    pallas_call x1, Pallas kernels, local(): pl.pallas_call(spread, out_shape=(jax.ShapeDtypeStruct((8, DIRS, rows), F...  1.75 us

profile of v2, /device:TPU:0, one launch (start us, length us, event | category | flops | bytes accessed | tf_op | source)
XLA Modules:
  0.0 51.1 jit_solution(11353260014981252619)
XLA Ops:
  0.6 48.7 %shard_map.130.result = f32[6,64,128]{2,1,0:T(8,128)} custom-call(f32[8,64,256]{2,1,0:T(8,128)} %bitcast.5, s32[64,256]{1,0:T(8,128)} %mask_ref.1, f32[3,64]{1,0:T(4,128)} %stations_ref.1, f32[2,1536]{1,0:T(2,128)} %dirs_ref.1, f32[1536]{0:T(1024)} %flux_ref.1, f32[2,1536]{1,0:T(2,128)} %pol_ref.1, f32[1536]{0:T(1024)} %index_ref.1, s32[1536]{0:T(1024)} %clusters_ref.1, ...), custom_call_target="tpu_custom_call" | custom-call | tf_op jit(solution)/shard_map/pallas_call | solution.py:424
  49.4 1.7 %shard_map.131 = (f32[8,16,64]{2,1,0:T(8,128)}, f32[8,16,64]{2,1,0:T(8,128)}, f32[4,8,16,64]{3,2,1,0:T(8,128)}) custom-call(f32[6,64,128]{2,1,0:T(8,128)} %shard_map.130.result), custom_call_target="tpu_custom_call" | custom-call | tf_op jit(solution)/shard_map/pallas_call | solution.py:472

commit v3 on v2

--- a/solution.py
+++ b/solution.py
@@ -10,6 +10,7 @@
 
 DIRS = 16
 LANES = 128
+BF16_ROWS = 16
 PENALTY = 40.0
 STEP_SIZE = 0.5
 MESH = pl.DeviceIdType.MESH
@@ -80,6 +81,7 @@
     cons_ref,
     result,
     near_all,
+    place_all,
     vis_send,
     vis_recv,
     base_all,
@@ -92,6 +94,7 @@
     sky_cols,
     jones_cols,
     jones_rows,
+    jones_far,
     place_rows,
     left_even,
     left_odd,
@@ -104,6 +107,8 @@
     grad_cols,
     near_ssem,
     near_rsem,
+    place_ssem,
+    place_rsem,
     vis_ssem,
     vis_rsem,
     norm_ssem,
@@ -155,9 +160,10 @@
         ]
 
     gains = gains_ref[...]
-    near_all[my_block, 0 : 8 * DIRS] = gains.reshape(8 * DIRS, rows)
-    near_all[my_block, 8 * DIRS : 8 * DIRS + 3] = stations_ref[...]
     own_jones = packed(gains)
+    near_all[my_block] = own_jones
+    place_all[my_block] = jnp.zeros((8, 2 * rows), F32)
+    place_all[my_block, 0:3, 0:rows] = stations_ref[...]
     base_all[my_band] = own_jones + packed(duals_ref[...])
 
     mask = mask_ref[...].astype(F32)
@@ -166,7 +172,7 @@
             first, second = vis_ref[2 * pair] * mask, vis_ref[2 * pair + 1] * mask
         else:
             first = second = mask
-        turned = jnp.concatenate([first, second], 0).T
+        turned = jnp.concatenate([first, second], 0).T.astype(BF16)
         for block in range(blocks):
             vis_send[block, pair] = turned[block * rows : (block + 1) * rows]
         if pair < 4:
@@ -175,6 +181,9 @@
         else:
             mask_sum[...] = first
     pl.semaphore_wait(barrier, blocks - 1 + bands - 1)
+    place_copies = to_blocks(
+        lambda peer: place_all.at[my_block], place_all, place_ssem, place_rsem
+    )
     near_copies = to_blocks(lambda peer: near_all.at[my_block], near_all, near_ssem, near_rsem)
     vis_copies = to_blocks(lambda peer: vis_send.at[peer], vis_recv, vis_ssem, vis_rsem)
     base_copies = to_bands(base_all, base_ssem, base_rsem)
@@ -230,15 +239,15 @@
     log_ratio = jnp.log(jnp.full((8, LANES), ratio, F32))[0:1]
     own_place = stations_ref[...].T
 
-    for copy in near_copies:
+    for copy in place_copies:
         copy.wait()
     for block in range(blocks):
-        cut = slice(block * rows, (block + 1) * rows)
-        jones_rows[:, :, cut] = near_all[block, 0 : 8 * DIRS].reshape(8, DIRS, rows)
-        place_rows[0:3, cut] = near_all[block, 8 * DIRS : 8 * DIRS + 3]
-
-    def geometry(l_value, m_value, places):
-        n_value = jnp.sqrt(1.0 - l_value * l_value - m_value * m_value) - 1.0
+        place_rows[:, block * rows : (block + 1) * rows] = place_all[block, :, 0:rows]
+
+    def n_less(l_value, m_value):
+        return jnp.sqrt(1.0 - l_value * l_value - m_value * m_value) - 1.0
+
+    def geometry(l_value, m_value, n_value, places):
         return ratio * (l_value * places[0] + m_value * places[1] + n_value * places[2])
 
     def build(k, left, right):
@@ -249,31 +258,57 @@
             row[4:5] * factor,
             (row[2:3] - row[3:4]) * factor,
         )
-        turns = geometry(row[0:1], row[1:2], [own_place[:, a : a + 1] for a in range(3)])
-        own_r, own_i = (value.astype(F32) for value in phasor(turns))
-        for at, weight in enumerate(weights):
-            left[at * rows : (at + 1) * rows, 0:LANES] = (own_r * weight).astype(BF16)
-            left[at * rows : (at + 1) * rows, LANES:] = (own_i * weight).astype(BF16)
-        col = sky_cols[k][0:span]
+        step = 2 * BF16_ROWS
+        for low in range(0, rows, step):
+            places = [own_place[low : low + step, a : a + 1] for a in range(3)]
+            turns = geometry(row[0:1], row[1:2], n_less(row[0:1], row[1:2]), places)
+            own_r, own_i = (value.astype(F32) for value in phasor(turns))
+            for at, weight in enumerate(weights):
+                cut = slice(at * rows + low, at * rows + low + step)
+                left[cut, 0:LANES] = (own_r * weight).astype(BF16)
+                left[cut, LANES:] = (own_i * weight).astype(BF16)
         places = [place_rows[a : a + 1, :] for a in range(3)]
-        far_r, far_i = phasor(geometry(col[:, 0:1], col[:, 1:2], places))
-        right[0:span, 0:total] = far_r
-        right[0:span, total:] = -far_i
-        right[LANES : LANES + span, 0:total] = far_i
-        right[LANES : LANES + span, total:] = far_r
+        low = 0
+        while low < span:
+            high = min(low + step, span)
+            l_col, m_col = sky_cols[k, low:high, 0:1], sky_cols[k, low:high, 1:2]
+            n_col = n_less(l_col, m_col)
+            for tile in range(0, total, LANES):
+                lanes = slice(tile, tile + LANES)
+                turns = geometry(l_col, m_col, n_col, [place[:, lanes] for place in places])
+                far_r, far_i = phasor(turns)
+                right[low:high, lanes] = far_r
+                right[low:high, total + tile : total + tile + LANES] = -far_i
+                right[LANES + low : LANES + high, lanes] = far_i
+                right[LANES + low : LANES + high, total + tile : total + tile + LANES] = far_r
+            low = high
 
     def multiply(k, left, right):
         coh[k] = jnp.dot(left[...], right[...], preferred_element_type=F32)
 
     build(0, left_even, right_even)
 
-    @pl.loop(0, DIRS // 2)
+    @pl.loop(0, DIRS // 2 - 1)
     def coherencies(at):
         build(2 * at + 1, left_odd, right_odd)
         multiply(2 * at, left_even, right_even)
-        build(jnp.minimum(2 * at + 2, DIRS - 1), left_even, right_even)
+        build(2 * at + 2, left_even, right_even)
         multiply(2 * at + 1, left_odd, right_odd)
 
+    build(DIRS - 1, left_odd, right_odd)
+    multiply(DIRS - 2, left_even, right_even)
+    multiply(DIRS - 1, left_odd, right_odd)
+
+    for copy in near_copies:
+        copy.wait()
+    for block in range(blocks):
+        cut = slice(block * rows, (block + 1) * rows)
+        near = near_all[block]
+        jones_rows[0:4, :, cut] = near[:, 0:rows].reshape(4, DIRS, rows)
+        jones_rows[4:8, :, cut] = near[:, rows:].reshape(4, DIRS, rows)
+    for k in range(DIRS):
+        for at in range(8):
+            jones_far[k, at] = jnp.broadcast_to(jones_rows[at, k : k + 1, :], (8, total))
     for copy in vis_copies:
         copy.wait()
     for i in range(2):
@@ -281,65 +316,82 @@
             for part in range(2):
                 lanes = slice(part * rows, (part + 1) * rows)
                 other = jnp.concatenate(
-                    [vis_recv[block, 2 * j + i, :, lanes] for block in range(blocks)], 1
+                    [vis_recv[block, 2 * j + i, :, lanes].astype(F32) for block in range(blocks)],
+                    1,
                 )
                 at = 2 * (2 * i + j) + part
                 wide[at] = wide[at] + other if part == 0 else wide[at] - other
-    mask_sum[...] += jnp.concatenate([vis_recv[block, 4, :, 0:rows] for block in range(blocks)], 1)
+    mask_sum[...] += jnp.concatenate(
+        [vis_recv[block, 4, :, 0:rows].astype(F32) for block in range(blocks)], 1
+    )
     lane = lax.broadcasted_iota(jnp.int32, (8, 8 * DIRS), 1)
 
     @pl.loop(0, rows // 8)
     def gradient(row_at):
         cut = pl.ds(pl.multiple_of(row_at * 8, 8), 8)
 
+        tiles = [slice(tile, tile + LANES) for tile in range(0, total, LANES)]
+
         def add_model(k, sums):
-            entries = []
-            for at in range(3):
-                rows_at = pl.ds(pl.multiple_of(at * rows + row_at * 8, 8), 8)
-                entries.append((coh[k, rows_at, 0:total], coh[k, rows_at, total:]))
-            matrix = ((entries[0], entries[1]), (entries[1], entries[2]))
             near = jones_cols[k, cut, :]
-            sums = list(sums)
-            for el in range(2):
-                far = [
-                    tuple(jones_rows[4 * el + 2 * n + a, pl.ds(k, 1), :] for a in range(2))
-                    for n in range(2)
-                ]
-                for m in range(2):
-                    (a_r, a_i), (b_r, b_i) = matrix[m]
-                    (c_r, c_i), (d_r, d_i) = far
-                    y_r = (a_r * c_r + a_i * c_i) + (b_r * d_r + b_i * d_i)
-                    y_i = (a_i * c_r - a_r * c_i) + (b_i * d_r - b_r * d_i)
-                    far_terms[k, 4 * m + 2 * el] = y_r
-                    far_terms[k, 4 * m + 2 * el + 1] = y_i
-                    for i in range(2):
-                        p_r = near[:, 4 * i + 2 * m : 4 * i + 2 * m + 1]
-                        p_i = near[:, 4 * i + 2 * m + 1 : 4 * i + 2 * m + 2]
-                        at = 4 * i + 2 * el
-                        sums[at] = sums[at] + (p_r * y_r - p_i * y_i)
-                        sums[at + 1] = sums[at + 1] + (p_r * y_i + p_i * y_r)
-            return tuple(sums)
+            near = [jnp.broadcast_to(near[:, at : at + 1], (8, LANES)) for at in range(8)]
+            done = []
+            for tile, lanes in enumerate(tiles):
+                far_lanes = slice(total + tile * LANES, total + (tile + 1) * LANES)
+                entries = []
+                for at in range(3):
+                    rows_at = pl.ds(pl.multiple_of(at * rows + row_at * 8, 8), 8)
+                    entries.append((coh[k, rows_at, lanes], coh[k, rows_at, far_lanes]))
+                matrix = ((entries[0], entries[1]), (entries[1], entries[2]))
+                own = list(sums[8 * tile : 8 * tile + 8])
+                for el in range(2):
+                    c_r, c_i, d_r, d_i = (jones_far[k, 4 * el + a, :, lanes] for a in range(4))
+                    for m in range(2):
+                        (a_r, a_i), (b_r, b_i) = matrix[m]
+                        y_r = (a_r * c_r + a_i * c_i) + (b_r * d_r + b_i * d_i)
+                        y_i = (a_i * c_r - a_r * c_i) + (b_i * d_r - b_r * d_i)
+                        far_terms[k, 4 * m + 2 * el, :, lanes] = y_r
+                        far_terms[k, 4 * m + 2 * el + 1, :, lanes] = y_i
+                        for i in range(2):
+                            p_r, p_i = near[4 * i + 2 * m], near[4 * i + 2 * m + 1]
+                            at = 4 * i + 2 * el
+                            own[at] = own[at] + (p_r * y_r - p_i * y_i)
+                            own[at + 1] = own[at + 1] + (p_r * y_i + p_i * y_r)
+                done += own
+            return tuple(done)
 
         sums = lax.fori_loop(
-            0, DIRS, add_model, tuple(jnp.zeros((8, total), F32) for _ in range(8)), unroll=2
+            0,
+            DIRS,
+            add_model,
+            tuple(jnp.zeros((8, LANES), F32) for _ in range(8 * len(tiles))),
+            unroll=2,
         )
-        both = mask_sum[cut]
-        w = [wide[at, cut] - both * sums[at] for at in range(8)]
+        w = [
+            [
+                wide[at, cut, lanes] - mask_sum[cut, lanes] * sums[8 * tile + at]
+                for at in range(8)
+            ]
+            for tile, lanes in enumerate(tiles)
+        ]
 
         def add_gradient(k, columns):
-            y = [far_terms[k, at] for at in range(8)]
-            for i in range(2):
-                for j in range(2):
-                    real = imag = None
-                    for m in range(2):
-                        w_r, w_i = w[4 * i + 2 * m], w[4 * i + 2 * m + 1]
-                        y_r, y_i = y[4 * j + 2 * m], y[4 * j + 2 * m + 1]
-                        one, two = w_r * y_r + w_i * y_i, w_i * y_r - w_r * y_i
-                        real, imag = (one, two) if m == 0 else (real + one, imag + two)
-                    for part, member_sum in enumerate((real, imag)):
-                        place = (4 * i + 2 * j + part) * DIRS + k
-                        summed = jnp.sum(member_sum, 1, keepdims=True)
-                        columns = jnp.where(lane == place, summed, columns)
+            totals = [None] * 8
+            for tile, lanes in enumerate(tiles):
+                y = [far_terms[k, at, :, lanes] for at in range(8)]
+                for i in range(2):
+                    for j in range(2):
+                        at = 4 * i + 2 * j
+                        for m in range(2):
+                            w_r, w_i = w[tile][4 * i + 2 * m], w[tile][4 * i + 2 * m + 1]
+                            y_r, y_i = y[4 * j + 2 * m], y[4 * j + 2 * m + 1]
+                            both = (w_r * y_r + w_i * y_i, w_i * y_r - w_r * y_i)
+                            for part in range(2):
+                                old = totals[at + part]
+                                totals[at + part] = both[part] if old is None else old + both[part]
+            for at in range(8):
+                summed = jnp.sum(totals[at], 1, keepdims=True)
+                columns = jnp.where(lane == at * DIRS + k, summed, columns)
             return columns
 
         grad_cols[cut] = lax.fori_loop(
@@ -427,9 +479,10 @@
         in_specs=[vmem] * 11,
         out_specs=vmem,
         scratch_shapes=[
-            pltpu.VMEM((blocks, 8 * DIRS + 8, rows), F32),
-            pltpu.VMEM((blocks, 5, rows, 2 * rows), F32),
-            pltpu.VMEM((blocks, 5, rows, 2 * rows), F32),
+            pltpu.VMEM((blocks, 4 * DIRS, 2 * rows), F32),
+            pltpu.VMEM((blocks, 8, 2 * rows), F32),
+            pltpu.VMEM((blocks, 5, rows, 2 * rows), BF16),
+            pltpu.VMEM((blocks, 5, rows, 2 * rows), BF16),
             pltpu.VMEM((bands, 4 * DIRS, 2 * rows), F32),
             pltpu.VMEM((bands, 4 * DIRS, 2 * rows), F32),
             pltpu.VMEM((blocks, 8, 2 * rows), F32),
@@ -440,6 +493,7 @@
             pltpu.VMEM((DIRS, LANES, 8), F32),
             pltpu.VMEM((DIRS, rows, 8), F32),
             pltpu.VMEM((8, DIRS, total), F32),
+            pltpu.VMEM((DIRS, 8, 8, total), F32),
             pltpu.VMEM((8, total), F32),
             pltpu.VMEM((3 * rows, 2 * LANES), BF16),
             pltpu.VMEM((3 * rows, 2 * LANES), BF16),
@@ -451,7 +505,7 @@
             pltpu.VMEM((rows, total), F32),
             pltpu.VMEM((rows, 8 * DIRS), F32),
         ]
-        + [block_sem] * 6
+        + [block_sem] * 8
         + [band_sem] * 6,
         compiler_params=pltpu.CompilerParams(
             collective_id=0, has_side_effects=True, vmem_limit_bytes=58 * 1024 * 1024

time: 51.3 us -> 41.6 us (0.81)
  Pallas kernels: 50.5 us -> 40.8 us
    pallas_call x1, Pallas kernels: 48.7 us -> 39 us  [local(): pl.pallas_call(functools.partial(kernel, bands, blocks), out_shape=jax.Sh...]
where the time goes in v3:
time: 41.6 us; the launch traced here: 41.4 us
  Pallas kernels  40.8 us (98%)
  between operations  0.64 us (2%)
    pallas_call x1, Pallas kernels, local(): pl.pallas_call(functools.partial(kernel, bands, blocks), out_shape=jax.Sh...  39 us
    pallas_call x1, Pallas kernels, local(): pl.pallas_call(spread, out_shape=(jax.ShapeDtypeStruct((8, DIRS, rows), F...  1.75 us

profile of v3, /device:TPU:0, one launch (start us, length us, event | category | flops | bytes accessed | tf_op | source)
XLA Modules:
  0.0 41.4 jit_solution(2753000946317350412)
XLA Ops:
  0.6 39.0 %shard_map.130.result = f32[6,64,128]{2,1,0:T(8,128)} custom-call(f32[8,64,256]{2,1,0:T(8,128)} %bitcast.5, s32[64,256]{1,0:T(8,128)} %mask_ref.1, f32[3,64]{1,0:T(4,128)} %stations_ref.1, f32[2,1536]{1,0:T(2,128)} %dirs_ref.1, f32[1536]{0:T(1024)} %flux_ref.1, f32[2,1536]{1,0:T(2,128)} %pol_ref.1, f32[1536]{0:T(1024)} %index_ref.1, s32[1536]{0:T(1024)} %clusters_ref.1, ...), custom_call_target="tpu_custom_call" | custom-call | tf_op jit(solution)/shard_map/pallas_call | solution.py:476
  39.7 1.7 %shard_map.131 = (f32[8,16,64]{2,1,0:T(8,128)}, f32[8,16,64]{2,1,0:T(8,128)}, f32[4,8,16,64]{3,2,1,0:T(8,128)}) custom-call(f32[6,64,128]{2,1,0:T(8,128)} %shard_map.130.result), custom_call_target="tpu_custom_call" | custom-call | tf_op jit(solution)/shard_map/pallas_call | solution.py:526

commit v4 on v3

--- a/solution.py
+++ b/solution.py
@@ -59,10 +59,8 @@
     return horner(COS_SERIES, square).astype(BF16), (horner(SIN_SERIES, square) * part).astype(BF16)
 
 
-def packed(value):
-    half = value.shape[0] // 2
-    rows, cols = half * value.shape[1], value.shape[2]
-    return jnp.concatenate([value[:half].reshape(rows, cols), value[half:].reshape(rows, cols)], 1)
+def by_station(value):
+    return value.reshape(8 * DIRS, value.shape[2]).T
 
 
 def kernel(
@@ -87,7 +85,6 @@
     base_all,
     drive_all,
     norm_all,
-    step_all,
     oh_rank,
     sky_lhs,
     sky_rows,
@@ -96,13 +93,13 @@
     jones_rows,
     jones_far,
     place_rows,
-    left_even,
-    left_odd,
+    left_all,
     right_even,
     right_odd,
     coh,
     far_terms,
     wide,
+    model,
     mask_sum,
     grad_cols,
     near_ssem,
@@ -117,8 +114,6 @@
     base_rsem,
     drive_ssem,
     drive_rsem,
-    step_ssem,
-    step_rsem,
 ):
     my_band = lax.axis_index("freq")
     my_block = lax.axis_index("stn")
@@ -130,10 +125,18 @@
     barrier = pltpu.get_barrier_semaphore()
     stn_peers = [lax.rem(my_block + d, blocks) for d in range(1, blocks)]
     freq_peers = [lax.rem(my_band + d, bands) for d in range(1, bands)]
-    for peer in stn_peers:
-        pl.semaphore_signal(barrier, inc=1, device_id=(my_band, peer), device_id_type=MESH)
-    for peer in freq_peers:
-        pl.semaphore_signal(barrier, inc=1, device_id=(peer, my_block), device_id_type=MESH)
+    slots = bands * blocks
+    my_slot = my_band * blocks + my_block
+
+    def slot_device(distance):
+        slot = lax.rem(my_slot + distance, slots)
+        return (slot // blocks, lax.rem(slot, blocks))
+
+    @pl.loop(1, slots)
+    def greet(distance):
+        pl.semaphore_signal(
+            barrier, inc=1, device_id=slot_device(distance), device_id_type=MESH
+        )
 
     def send(source, target, ssem, rsem, at, device):
         copy = pltpu.make_async_remote_copy(
@@ -153,18 +156,31 @@
             for at, peer in enumerate(stn_peers)
         ]
 
-    def to_bands(target, ssem, rsem):
-        own = target.at[my_band]
+    def to_bands(target, ssem, rsem, first=0):
         return [
-            send(own, own, ssem, rsem, at, (peer, my_block)) for at, peer in enumerate(freq_peers)
+            send(target, target, ssem, rsem, first + at, (peer, my_block))
+            for at, peer in enumerate(freq_peers)
         ]
 
+    def norm_copy(distance):
+        return pltpu.make_async_remote_copy(
+            src_ref=norm_all.at[my_slot],
+            dst_ref=norm_all.at[my_slot],
+            send_sem=norm_ssem.at[distance],
+            recv_sem=norm_rsem.at[distance],
+            device_id=slot_device(distance),
+            device_id_type=MESH,
+        )
+
     gains = gains_ref[...]
-    own_jones = packed(gains)
-    near_all[my_block] = own_jones
+    half = 4 * DIRS
+    near_all[my_block] = jnp.concatenate(
+        [gains[0:4].reshape(half, rows), gains[4:8].reshape(half, rows)], 1
+    )
+    own_jones = by_station(gains)
     place_all[my_block] = jnp.zeros((8, 2 * rows), F32)
     place_all[my_block, 0:3, 0:rows] = stations_ref[...]
-    base_all[my_band] = own_jones + packed(duals_ref[...])
+    base_all[my_band] = own_jones + by_station(duals_ref[...])
 
     mask = mask_ref[...].astype(F32)
     for pair in range(5):
@@ -180,13 +196,13 @@
             wide[2 * pair + 1] = second
         else:
             mask_sum[...] = first
-    pl.semaphore_wait(barrier, blocks - 1 + bands - 1)
+    pl.semaphore_wait(barrier, slots - 1)
     place_copies = to_blocks(
         lambda peer: place_all.at[my_block], place_all, place_ssem, place_rsem
     )
     near_copies = to_blocks(lambda peer: near_all.at[my_block], near_all, near_ssem, near_rsem)
     vis_copies = to_blocks(lambda peer: vis_send.at[peer], vis_recv, vis_ssem, vis_rsem)
-    base_copies = to_bands(base_all, base_ssem, base_rsem)
+    base_copies = to_bands(base_all.at[my_band], base_ssem, base_rsem)
     vis_recv[my_block] = vis_send[my_block]
 
     clusters = clusters_ref[...].reshape(1, comps)
@@ -239,18 +255,14 @@
     log_ratio = jnp.log(jnp.full((8, LANES), ratio, F32))[0:1]
     own_place = stations_ref[...].T
 
-    for copy in place_copies:
-        copy.wait()
-    for block in range(blocks):
-        place_rows[:, block * rows : (block + 1) * rows] = place_all[block, :, 0:rows]
-
     def n_less(l_value, m_value):
         return jnp.sqrt(1.0 - l_value * l_value - m_value * m_value) - 1.0
 
     def geometry(l_value, m_value, n_value, places):
         return ratio * (l_value * places[0] + m_value * places[1] + n_value * places[2])
 
-    def build(k, left, right):
+    @pl.loop(0, DIRS)
+    def build_left(k):
         row = sky_rows[k]
         factor = jnp.exp(row[5:6] * log_ratio)
         weights = (
@@ -265,8 +277,16 @@
             own_r, own_i = (value.astype(F32) for value in phasor(turns))
             for at, weight in enumerate(weights):
                 cut = slice(at * rows + low, at * rows + low + step)
-                left[cut, 0:LANES] = (own_r * weight).astype(BF16)
-                left[cut, LANES:] = (own_i * weight).astype(BF16)
+                left_all[k, cut, 0:LANES] = (own_r * weight).astype(BF16)
+                left_all[k, cut, LANES:] = (own_i * weight).astype(BF16)
+
+    for copy in place_copies:
+        copy.wait()
+    for block in range(blocks):
+        place_rows[:, block * rows : (block + 1) * rows] = place_all[block, :, 0:rows]
+
+    def build(k, right):
+        step = 2 * BF16_ROWS
         places = [place_rows[a : a + 1, :] for a in range(3)]
         low = 0
         while low < span:
@@ -283,21 +303,21 @@
                 right[LANES + low : LANES + high, total + tile : total + tile + LANES] = far_r
             low = high
 
-    def multiply(k, left, right):
-        coh[k] = jnp.dot(left[...], right[...], preferred_element_type=F32)
-
-    build(0, left_even, right_even)
+    def multiply(k, right):
+        coh[k] = jnp.dot(left_all[k], right[...], preferred_element_type=F32)
+
+    build(0, right_even)
 
     @pl.loop(0, DIRS // 2 - 1)
     def coherencies(at):
-        build(2 * at + 1, left_odd, right_odd)
-        multiply(2 * at, left_even, right_even)
-        build(2 * at + 2, left_even, right_even)
-        multiply(2 * at + 1, left_odd, right_odd)
-
-    build(DIRS - 1, left_odd, right_odd)
-    multiply(DIRS - 2, left_even, right_even)
-    multiply(DIRS - 1, left_odd, right_odd)
+        build(2 * at + 1, right_odd)
+        multiply(2 * at, right_even)
+        build(2 * at + 2, right_even)
+        multiply(2 * at + 1, right_odd)
+
+    build(DIRS - 1, right_odd)
+    multiply(DIRS - 2, right_even)
+    multiply(DIRS - 1, right_odd)
 
     for copy in near_copies:
         copy.wait()
@@ -309,28 +329,31 @@
     for k in range(DIRS):
         for at in range(8):
             jones_far[k, at] = jnp.broadcast_to(jones_rows[at, k : k + 1, :], (8, total))
-    for copy in vis_copies:
-        copy.wait()
-    for i in range(2):
-        for j in range(2):
-            for part in range(2):
-                lanes = slice(part * rows, (part + 1) * rows)
-                other = jnp.concatenate(
-                    [vis_recv[block, 2 * j + i, :, lanes].astype(F32) for block in range(blocks)],
-                    1,
-                )
-                at = 2 * (2 * i + j) + part
-                wide[at] = wide[at] + other if part == 0 else wide[at] - other
-    mask_sum[...] += jnp.concatenate(
-        [vis_recv[block, 4, :, 0:rows].astype(F32) for block in range(blocks)], 1
-    )
+    def finish_wide():
+        for copy in vis_copies:
+            copy.wait()
+        for i in range(2):
+            for j in range(2):
+                for part in range(2):
+                    lanes = slice(part * rows, (part + 1) * rows)
+                    other = jnp.concatenate(
+                        [vis_recv[block, 2 * j + i, :, lanes].astype(F32) for block in range(blocks)],
+                        1,
+                    )
+                    at = 2 * (2 * i + j) + part
+                    wide[at] = wide[at] + other if part == 0 else wide[at] - other
+        mask_sum[...] += jnp.concatenate(
+            [vis_recv[block, 4, :, 0:rows].astype(F32) for block in range(blocks)], 1
+        )
+
     lane = lax.broadcasted_iota(jnp.int32, (8, 8 * DIRS), 1)
 
-    @pl.loop(0, rows // 8)
-    def gradient(row_at):
+    kept = far_terms.shape[2]
+    tiles = [slice(tile, tile + LANES) for tile in range(0, total, LANES)]
+
+    def model_rows(row_at):
         cut = pl.ds(pl.multiple_of(row_at * 8, 8), 8)
-
-        tiles = [slice(tile, tile + LANES) for tile in range(0, total, LANES)]
+        kept_cut = cut if kept == rows else slice(0, 8)
 
         def add_model(k, sums):
             near = jones_cols[k, cut, :]
@@ -350,8 +373,8 @@
                         (a_r, a_i), (b_r, b_i) = matrix[m]
                         y_r = (a_r * c_r + a_i * c_i) + (b_r * d_r + b_i * d_i)
                         y_i = (a_i * c_r - a_r * c_i) + (b_i * d_r - b_r * d_i)
-                        far_terms[k, 4 * m + 2 * el, :, lanes] = y_r
-                        far_terms[k, 4 * m + 2 * el + 1, :, lanes] = y_i
+                        far_terms[k, 4 * m + 2 * el, kept_cut, lanes] = y_r
+                        far_terms[k, 4 * m + 2 * el + 1, kept_cut, lanes] = y_i
                         for i in range(2):
                             p_r, p_i = near[4 * i + 2 * m], near[4 * i + 2 * m + 1]
                             at = 4 * i + 2 * el
@@ -367,18 +390,25 @@
             tuple(jnp.zeros((8, LANES), F32) for _ in range(8 * len(tiles))),
             unroll=2,
         )
+        for tile, lanes in enumerate(tiles):
+            for at in range(8):
+                model[at, cut, lanes] = sums[8 * tile + at]
+
+    def gradient_rows(row_at):
+        cut = pl.ds(pl.multiple_of(row_at * 8, 8), 8)
+        kept_cut = cut if kept == rows else slice(0, 8)
         w = [
             [
-                wide[at, cut, lanes] - mask_sum[cut, lanes] * sums[8 * tile + at]
+                wide[at, cut, lanes] - mask_sum[cut, lanes] * model[at, cut, lanes]
                 for at in range(8)
             ]
-            for tile, lanes in enumerate(tiles)
+            for lanes in tiles
         ]
 
         def add_gradient(k, columns):
             totals = [None] * 8
             for tile, lanes in enumerate(tiles):
-                y = [far_terms[k, at, :, lanes] for at in range(8)]
+                y = [far_terms[k, at, kept_cut, lanes] for at in range(8)]
                 for i in range(2):
                     for j in range(2):
                         at = 4 * i + 2 * j
@@ -405,30 +435,52 @@
         0.5 * (3.0 * centre * centre - 1.0),
         0.5 * (5.0 * centre * centre * centre - 3.0 * centre),
     )
-    poly = packed(cons_ref[0])
+    if kept == rows:
+        pl.loop(0, rows // 8)(model_rows)
+    poly = cons_ref[0]
     for i in range(1, 4):
-        poly = poly + basis[i] * packed(cons_ref[i])
-    base = base_all[my_band]
-    turned = grad_cols[...].T
-    grads = jnp.concatenate([turned[0 : 4 * DIRS], turned[4 * DIRS :]], 1)
-    drive = PENALTY / 2.0 * (base - poly) - grads
-    drive_all[my_band] = drive
-    norm_all[my_block] = jnp.sum((drive * drive).reshape(-1, 8, 2 * rows), 0)
-    norm_copies = to_blocks(lambda peer: norm_all.at[my_block], norm_all, norm_ssem, norm_rsem)
-    drive_copies = to_bands(drive_all, drive_ssem, drive_rsem)
-    for copy in norm_copies:
-        copy.wait()
-    squares = norm_all[0]
-    for block in range(1, blocks):
-        squares = squares + norm_all[block]
-    mean = jnp.sum(jnp.sum(squares, 0, keepdims=True), 1, keepdims=True) / (8 * DIRS * total)
-    step_all[my_band] = jnp.broadcast_to(STEP_SIZE / jnp.sqrt(mean + 1e-06), (8, 2 * rows))
-    step_copies = to_bands(step_all, step_ssem, step_rsem)
-    result[0] = own_jones - step_all[my_band, 0:1] * drive
-    for copy in base_copies + drive_copies + step_copies:
+        poly = poly + basis[i] * cons_ref[i]
+    pull = PENALTY / 2.0 * (base_all[my_band] - by_station(poly))
+    finish_wide()
+
+    drive_copies = []
+    squares = jnp.zeros((8, 8 * DIRS), F32)
+    for part in range(2):
+
+        @pl.loop(part * rows // 16, (part + 1) * rows // 16)
+        def gradient(row_at):
+            if kept != rows:
+                model_rows(row_at)
+            gradient_rows(row_at)
+
+        cut = slice(part * rows // 2, (part + 1) * rows // 2)
+        piece = pull[cut] - grad_cols[cut]
+        drive_all[my_band, cut] = piece
+        squares = squares + jnp.sum((piece * piece).reshape(-1, 8, 8 * DIRS), 0)
+        if part == 1:
+            norm_all[my_slot] = jnp.sum(squares, 0, keepdims=True)
+
+            @pl.loop(1, slots)
+            def send_norms(distance):
+                norm_copy(distance).start()
+
+        drive_copies += to_bands(
+            drive_all.at[my_band, cut], drive_ssem, drive_rsem, part * (bands - 1)
+        )
+
+    @pl.loop(1, slots)
+    def wait_norms(distance):
+        norm_copy(distance).wait()
+
+    squares = jnp.concatenate(
+        [jnp.sum(norm_all[band * blocks : (band + 1) * blocks], 0) for band in range(bands)], 0
+    )
+    mean = jnp.sum(squares, 1, keepdims=True) / (8 * DIRS * total)
+    steps = STEP_SIZE / jnp.sqrt(mean + 1e-06)
+    for copy in base_copies + drive_copies:
         copy.wait()
     sums = [
-        base_all[band] - step_all[band, 0:1] * drive_all[band] for band in range(bands)
+        base_all[band] - steps[band : band + 1] * drive_all[band] for band in range(bands)
     ]
     table = basis_rows(bands)
     solve = np.linalg.solve(table.T @ table, table.T)
@@ -439,18 +491,19 @@
             value = value + float(solve[i, band]) * sums[band]
         result[2 + i] = value
         fitted = value if i == 0 else fitted + basis[i] * value
-    result[1] = base - step_all[my_band, 0:1] * drive - fitted
+    squares = jnp.sum(norm_all[pl.ds(my_band * blocks, blocks)], 0)
+    mean = jnp.sum(squares, 1, keepdims=True) / (8 * DIRS * total)
+    jones_next = own_jones - STEP_SIZE / jnp.sqrt(mean + 1e-06) * drive_all[my_band]
+    result[0] = jones_next
+    result[1] = by_station(duals_ref[...]) + jones_next - fitted
 
 
 def spread(result, jones_out, duals_out, cons_out):
-    rows = jones_out.shape[2]
-    for part in range(2):
-        lanes = slice(part * rows, (part + 1) * rows)
-        cut = slice(4 * part, 4 * part + 4)
-        jones_out[cut] = result[0, :, lanes].reshape(4, DIRS, rows)
-        duals_out[cut] = result[1, :, lanes].reshape(4, DIRS, rows)
-        for i in range(4):
-            cons_out[i, cut] = result[2 + i, :, lanes].reshape(4, DIRS, rows)
+    shape = jones_out.shape
+    jones_out[...] = result[0].T.reshape(shape)
+    duals_out[...] = result[1].T.reshape(shape)
+    for i in range(4):
+        cons_out[i] = result[2 + i].T.reshape(shape)
 
 
 def local(
@@ -470,12 +523,13 @@
     blocks = lax.axis_size("stn")
     rows, total = flag_mask.shape
     comps = clusters.shape[0]
+    kept = rows if DIRS * 8 * rows * total * 4 <= 2**24 else 8
     vmem = pl.BlockSpec(memory_space=pltpu.VMEM)
     block_sem = pltpu.SemaphoreType.DMA((blocks - 1,))
     band_sem = pltpu.SemaphoreType.DMA((bands - 1,))
     result = pl.pallas_call(
         functools.partial(kernel, bands, blocks),
-        out_shape=jax.ShapeDtypeStruct((6, 4 * DIRS, 2 * rows), F32),
+        out_shape=jax.ShapeDtypeStruct((6, rows, 8 * DIRS), F32),
         in_specs=[vmem] * 11,
         out_specs=vmem,
         scratch_shapes=[
@@ -483,10 +537,9 @@
             pltpu.VMEM((blocks, 8, 2 * rows), F32),
             pltpu.VMEM((blocks, 5, rows, 2 * rows), BF16),
             pltpu.VMEM((blocks, 5, rows, 2 * rows), BF16),
-            pltpu.VMEM((bands, 4 * DIRS, 2 * rows), F32),
-            pltpu.VMEM((bands, 4 * DIRS, 2 * rows), F32),
-            pltpu.VMEM((blocks, 8, 2 * rows), F32),
-            pltpu.VMEM((bands, 8, 2 * rows), F32),
+            pltpu.VMEM((bands, rows, 8 * DIRS), F32),
+            pltpu.VMEM((bands, rows, 8 * DIRS), F32),
+            pltpu.VMEM((bands * blocks, 1, 8 * DIRS), F32),
             pltpu.VMEM((LANES, comps), BF16),
             pltpu.VMEM((32 * DIRS, comps), BF16),
             pltpu.VMEM((DIRS, 8, LANES), F32),
@@ -495,18 +548,20 @@
             pltpu.VMEM((8, DIRS, total), F32),
             pltpu.VMEM((DIRS, 8, 8, total), F32),
             pltpu.VMEM((8, total), F32),
-            pltpu.VMEM((3 * rows, 2 * LANES), BF16),
-            pltpu.VMEM((3 * rows, 2 * LANES), BF16),
+            pltpu.VMEM((DIRS, 3 * rows, 2 * LANES), BF16),
             pltpu.VMEM((2 * LANES, 2 * total), BF16),
             pltpu.VMEM((2 * LANES, 2 * total), BF16),
             pltpu.VMEM((DIRS, 3 * rows, 2 * total), F32),
-            pltpu.VMEM((DIRS, 8, 8, total), F32),
+            pltpu.VMEM((DIRS, 8, kept, total), F32),
+            pltpu.VMEM((8, rows, total), F32),
             pltpu.VMEM((8, rows, total), F32),
             pltpu.VMEM((rows, total), F32),
             pltpu.VMEM((rows, 8 * DIRS), F32),
         ]
-        + [block_sem] * 8
-        + [band_sem] * 6,
+        + [block_sem] * 6
+        + [pltpu.SemaphoreType.DMA((bands * blocks,))] * 2
+        + [band_sem] * 2
+        + [pltpu.SemaphoreType.DMA((2 * (bands - 1),))] * 2,
         compiler_params=pltpu.CompilerParams(
             collective_id=0, has_side_effects=True, vmem_limit_bytes=58 * 1024 * 1024
         ),

time: 41.6 us -> 37.7 us (0.906)
  Pallas kernels: 40.8 us -> 36.9 us
    pallas_call x1, Pallas kernels: 39 us -> 35.1 us  [local(): pl.pallas_call(functools.partial(kernel, bands, blocks), out_shape=jax.Sh...]
where the time goes in v4:
time: 37.7 us; the launch traced here: 37.5 us
  Pallas kernels  36.9 us (98%)
  between operations  0.64 us (2%)
    pallas_call x1, Pallas kernels, local(): pl.pallas_call(functools.partial(kernel, bands, blocks), out_shape=jax.Sh...  35.1 us
    pallas_call x1, Pallas kernels, local(): pl.pallas_call(spread, out_shape=(jax.ShapeDtypeStruct((8, DIRS, rows), F...  1.8 us

profile of v4, /device:TPU:0, one launch (start us, length us, event | category | flops | bytes accessed | tf_op | source)
XLA Modules:
  0.0 37.5 jit_solution(17151541405905924486)
XLA Ops:
  0.6 35.1 %shard_map.130.result = f32[6,64,128]{2,1,0:T(8,128)} custom-call(f32[8,64,256]{2,1,0:T(8,128)} %bitcast.5, s32[64,256]{1,0:T(8,128)} %mask_ref.1, f32[3,64]{1,0:T(4,128)} %stations_ref.1, f32[2,1536]{1,0:T(2,128)} %dirs_ref.1, f32[1536]{0:T(1024)} %flux_ref.1, f32[2,1536]{1,0:T(2,128)} %pol_ref.1, f32[1536]{0:T(1024)} %index_ref.1, s32[1536]{0:T(1024)} %clusters_ref.1, ...), custom_call_target="tpu_custom_call" | custom-call | tf_op jit(solution)/shard_map/pallas_call | solution.py:530
  35.7 1.8 %shard_map.131 = (f32[8,16,64]{2,1,0:T(8,128)}, f32[8,16,64]{2,1,0:T(8,128)}, f32[4,8,16,64]{3,2,1,0:T(8,128)}) custom-call(f32[6,64,128]{2,1,0:T(8,128)} %shard_map.130.result), custom_call_target="tpu_custom_call" | custom-call | tf_op jit(solution)/shard_map/pallas_call | solution.py:581

commit v5 on v4

--- a/solution.py
+++ b/solution.py
@@ -30,7 +30,7 @@
     return fits
 
 
-COS_SERIES, SIN_SERIES = turn_series(7)
+COS_SERIES, SIN_SERIES = turn_series(6)
 
 
 def basis_rows(band_count):
@@ -90,6 +90,7 @@
     sky_rows,
     sky_cols,
     jones_cols,
+    jones_near,
     jones_rows,
     jones_far,
     place_rows,
@@ -241,8 +242,20 @@
         sky_lhs[...], oh_rank[...], (((1,), (1,)), ((), ())), preferred_element_type=F32
     ).reshape(DIRS, 4, 8, LANES)
     sky = (sky[:, 2] + sky[:, 1]) + sky[:, 0]
-    sky_rows[...] = sky
-    sky_turned = sky.reshape(DIRS * 8, LANES).T
+    band_number = my_band.astype(F32)
+    ratio = 0.5 + 3.0 * (band_number + 0.5) / bands
+    l_all, m_all, i_all, q_all, u_all, slope = (sky[:, at] for at in range(6))
+    factor = jnp.exp(slope * jnp.log(jnp.full((DIRS, LANES), ratio, F32)))
+    n_all = jnp.sqrt(1.0 - l_all * l_all - m_all * m_all) - 1.0
+    sky_rows[:, 0] = l_all
+    sky_rows[:, 1] = m_all
+    sky_rows[:, 2] = n_all
+    sky_rows[:, 3] = (i_all + q_all) * factor
+    sky_rows[:, 4] = u_all * factor
+    sky_rows[:, 5] = (i_all - q_all) * factor
+    sky_rows[:, 6] = n_all
+    sky_rows[:, 7] = n_all
+    sky_turned = sky_rows[...].reshape(DIRS * 8, LANES).T
     for k in range(DIRS):
         sky_cols[k] = sky_turned[:, 8 * k : 8 * k + 8]
         jones_cols[k] = gains[:, k, :].T
@@ -250,32 +263,24 @@
     for right in (right_even, right_odd):
         right[span:LANES] = zero_rows
         right[LANES + span :] = zero_rows
-    band_number = my_band.astype(F32)
-    ratio = 0.5 + 3.0 * (band_number + 0.5) / bands
-    log_ratio = jnp.log(jnp.full((8, LANES), ratio, F32))[0:1]
-    own_place = stations_ref[...].T
-
-    def n_less(l_value, m_value):
-        return jnp.sqrt(1.0 - l_value * l_value - m_value * m_value) - 1.0
+    own_place = stations_ref[...].T * ratio
 
     def geometry(l_value, m_value, n_value, places):
-        return ratio * (l_value * places[0] + m_value * places[1] + n_value * places[2])
+        return l_value * places[0] + m_value * places[1] + n_value * places[2]
 
     @pl.loop(0, DIRS)
     def build_left(k):
         row = sky_rows[k]
-        factor = jnp.exp(row[5:6] * log_ratio)
-        weights = (
-            (row[2:3] + row[3:4]) * factor,
-            row[4:5] * factor,
-            (row[2:3] - row[3:4]) * factor,
-        )
+        near = jones_cols[k]
+        for at in range(8):
+            jones_near[k, at] = jnp.broadcast_to(near[:, at : at + 1], (rows, LANES))
         step = 2 * BF16_ROWS
         for low in range(0, rows, step):
             places = [own_place[low : low + step, a : a + 1] for a in range(3)]
-            turns = geometry(row[0:1], row[1:2], n_less(row[0:1], row[1:2]), places)
+            turns = geometry(row[0:1], row[1:2], row[2:3], places)
             own_r, own_i = (value.astype(F32) for value in phasor(turns))
-            for at, weight in enumerate(weights):
+            for at in range(3):
+                weight = row[3 + at : 4 + at]
                 cut = slice(at * rows + low, at * rows + low + step)
                 left_all[k, cut, 0:LANES] = (own_r * weight).astype(BF16)
                 left_all[k, cut, LANES:] = (own_i * weight).astype(BF16)
@@ -283,7 +288,7 @@
     for copy in place_copies:
         copy.wait()
     for block in range(blocks):
-        place_rows[:, block * rows : (block + 1) * rows] = place_all[block, :, 0:rows]
+        place_rows[:, block * rows : (block + 1) * rows] = place_all[block, :, 0:rows] * ratio
 
     def build(k, right):
         step = 2 * BF16_ROWS
@@ -291,8 +296,7 @@
         low = 0
         while low < span:
             high = min(low + step, span)
-            l_col, m_col = sky_cols[k, low:high, 0:1], sky_cols[k, low:high, 1:2]
-            n_col = n_less(l_col, m_col)
+            l_col, m_col, n_col = (sky_cols[k, low:high, at : at + 1] for at in range(3))
             for tile in range(0, total, LANES):
                 lanes = slice(tile, tile + LANES)
                 turns = geometry(l_col, m_col, n_col, [place[:, lanes] for place in places])
@@ -356,8 +360,7 @@
         kept_cut = cut if kept == rows else slice(0, 8)
 
         def add_model(k, sums):
-            near = jones_cols[k, cut, :]
-            near = [jnp.broadcast_to(near[:, at : at + 1], (8, LANES)) for at in range(8)]
+            near = [jones_near[k, at, cut] for at in range(8)]
             done = []
             for tile, lanes in enumerate(tiles):
                 far_lanes = slice(total + tile * LANES, total + (tile + 1) * LANES)
@@ -388,7 +391,7 @@
             DIRS,
             add_model,
             tuple(jnp.zeros((8, LANES), F32) for _ in range(8 * len(tiles))),
-            unroll=2,
+            unroll=4,
         )
         for tile, lanes in enumerate(tiles):
             for at in range(8):
@@ -425,7 +428,7 @@
             return columns
 
         grad_cols[cut] = lax.fori_loop(
-            0, DIRS, add_gradient, jnp.zeros((8, 8 * DIRS), F32), unroll=4
+            0, DIRS, add_gradient, jnp.zeros((8, 8 * DIRS), F32), unroll=8
         )
 
     centre = (2.0 * band_number + 1.0) / bands - 1.0
@@ -545,6 +548,7 @@
             pltpu.VMEM((DIRS, 8, LANES), F32),
             pltpu.VMEM((DIRS, LANES, 8), F32),
             pltpu.VMEM((DIRS, rows, 8), F32),
+            pltpu.VMEM((DIRS, 8, rows, LANES), F32),
             pltpu.VMEM((8, DIRS, total), F32),
             pltpu.VMEM((DIRS, 8, 8, total), F32),
             pltpu.VMEM((8, total), F32),

time: 37.7 us -> 33.2 us (0.88)
  Pallas kernels: 36.9 us -> 32.3 us
    pallas_call x1, Pallas kernels: 35.1 us -> 30.5 us  [local(): pl.pallas_call(functools.partial(kernel, bands, blocks), out_shape=jax.Sh...]
where the time goes in v5:
time: 33.2 us; the launch traced here: 33 us
  Pallas kernels  32.3 us (97%)
  between operations  0.64 us (2%)
    pallas_call x1, Pallas kernels, local(): pl.pallas_call(functools.partial(kernel, bands, blocks), out_shape=jax.Sh...  30.5 us
    pallas_call x1, Pallas kernels, local(): pl.pallas_call(spread, out_shape=(jax.ShapeDtypeStruct((8, DIRS, rows), F...  1.8 us

profile of v5, /device:TPU:0, one launch (start us, length us, event | category | flops | bytes accessed | tf_op | source)
XLA Modules:
  0.0 33.0 jit_solution(16644932018897734380)
XLA Ops:
  0.6 30.5 %shard_map.130.result = f32[6,64,128]{2,1,0:T(8,128)} custom-call(f32[8,64,256]{2,1,0:T(8,128)} %bitcast.5, s32[64,256]{1,0:T(8,128)} %mask_ref.1, f32[3,64]{1,0:T(4,128)} %stations_ref.1, f32[2,1536]{1,0:T(2,128)} %dirs_ref.1, f32[1536]{0:T(1024)} %flux_ref.1, f32[2,1536]{1,0:T(2,128)} %pol_ref.1, f32[1536]{0:T(1024)} %index_ref.1, s32[1536]{0:T(1024)} %clusters_ref.1, ...), custom_call_target="tpu_custom_call" | custom-call | tf_op jit(solution)/shard_map/pallas_call | solution.py:533
  31.2 1.8 %shard_map.131 = (f32[8,16,64]{2,1,0:T(8,128)}, f32[8,16,64]{2,1,0:T(8,128)}, f32[4,8,16,64]{3,2,1,0:T(8,128)}) custom-call(f32[6,64,128]{2,1,0:T(8,128)} %shard_map.130.result), custom_call_target="tpu_custom_call" | custom-call | tf_op jit(solution)/shard_map/pallas_call | solution.py:585

commit v6 on v5

--- a/solution.py
+++ b/solution.py
@@ -133,7 +133,14 @@
         slot = lax.rem(my_slot + distance, slots)
         return (slot // blocks, lax.rem(slot, blocks))
 
-    @pl.loop(1, slots)
+    def each_distance(act):
+        if slots <= 32:
+            for distance in range(1, slots):
+                act(distance)
+        else:
+            pl.loop(1, slots)(act)
+
+    @each_distance
     def greet(distance):
         pl.semaphore_signal(
             barrier, inc=1, device_id=slot_device(distance), device_id_type=MESH
@@ -268,7 +275,7 @@
     def geometry(l_value, m_value, n_value, places):
         return l_value * places[0] + m_value * places[1] + n_value * places[2]
 
-    @pl.loop(0, DIRS)
+    @pl.loop(0, DIRS, unroll=4)
     def build_left(k):
         row = sky_rows[k]
         near = jones_cols[k]
@@ -391,7 +398,7 @@
             DIRS,
             add_model,
             tuple(jnp.zeros((8, LANES), F32) for _ in range(8 * len(tiles))),
-            unroll=4,
+            unroll=8,
         )
         for tile, lanes in enumerate(tiles):
             for at in range(8):
@@ -428,7 +435,7 @@
             return columns
 
         grad_cols[cut] = lax.fori_loop(
-            0, DIRS, add_gradient, jnp.zeros((8, 8 * DIRS), F32), unroll=8
+            0, DIRS, add_gradient, jnp.zeros((8, 8 * DIRS), F32), unroll=16
         )
 
     centre = (2.0 * band_number + 1.0) / bands - 1.0
@@ -463,7 +470,7 @@
         if part == 1:
             norm_all[my_slot] = jnp.sum(squares, 0, keepdims=True)
 
-            @pl.loop(1, slots)
+            @each_distance
             def send_norms(distance):
                 norm_copy(distance).start()
 
@@ -471,7 +478,7 @@
             drive_all.at[my_band, cut], drive_ssem, drive_rsem, part * (bands - 1)
         )
 
-    @pl.loop(1, slots)
+    @each_distance
     def wait_norms(distance):
         norm_copy(distance).wait()
 
@@ -496,9 +503,9 @@
         fitted = value if i == 0 else fitted + basis[i] * value
     squares = jnp.sum(norm_all[pl.ds(my_band * blocks, blocks)], 0)
     mean = jnp.sum(squares, 1, keepdims=True) / (8 * DIRS * total)
-    jones_next = own_jones - STEP_SIZE / jnp.sqrt(mean + 1e-06) * drive_all[my_band]
-    result[0] = jones_next
-    result[1] = by_station(duals_ref[...]) + jones_next - fitted
+    move = STEP_SIZE / jnp.sqrt(mean + 1e-06) * drive_all[my_band]
+    result[0] = own_jones - move
+    result[1] = base_all[my_band] - move - fitted
 
 
 def spread(result, jones_out, duals_out, cons_out):

time: 33.2 us -> 31.9 us (0.961)
  Pallas kernels: 32.3 us -> 31.1 us
    pallas_call x1, Pallas kernels: 30.5 us -> 29.3 us  [local(): pl.pallas_call(functools.partial(kernel, bands, blocks), out_shape=jax.Sh...]
where the time goes in v6:
time: 31.9 us; the launch traced here: 31.8 us
  Pallas kernels  31.1 us (97%)
  between operations  0.64 us (2%)
    pallas_call x1, Pallas kernels, local(): pl.pallas_call(functools.partial(kernel, bands, blocks), out_shape=jax.Sh...  29.3 us
    pallas_call x1, Pallas kernels, local(): pl.pallas_call(spread, out_shape=(jax.ShapeDtypeStruct((8, DIRS, rows), F...  1.8 us

profile of v6, /device:TPU:0, one launch (start us, length us, event | category | flops | bytes accessed | tf_op | source)
XLA Modules:
  0.0 31.8 jit_solution(15855357739314465248)
XLA Ops:
  0.6 29.3 %shard_map.130.result = f32[6,64,128]{2,1,0:T(8,128)} custom-call(f32[8,64,256]{2,1,0:T(8,128)} %bitcast.5, s32[64,256]{1,0:T(8,128)} %mask_ref.1, f32[3,64]{1,0:T(4,128)} %stations_ref.1, f32[2,1536]{1,0:T(2,128)} %dirs_ref.1, f32[1536]{0:T(1024)} %flux_ref.1, f32[2,1536]{1,0:T(2,128)} %pol_ref.1, f32[1536]{0:T(1024)} %index_ref.1, s32[1536]{0:T(1024)} %clusters_ref.1, ...), custom_call_target="tpu_custom_call" | custom-call | tf_op jit(solution)/shard_map/pallas_call | solution.py:540
  30.0 1.8 %shard_map.131 = (f32[8,16,64]{2,1,0:T(8,128)}, f32[8,16,64]{2,1,0:T(8,128)}, f32[4,8,16,64]{3,2,1,0:T(8,128)}) custom-call(f32[6,64,128]{2,1,0:T(8,128)} %shard_map.130.result), custom_call_target="tpu_custom_call" | custom-call | tf_op jit(solution)/shard_map/pallas_call | solution.py:592
